TPU v7x, 128 devices: a whole 4x4x4 slice. The times are simulated.
128 devices in a mesh: block: 16 (over z_hi, x, core), line: 8 (over z_lo, y).
Axes of the slice: x: 4, y: 4, z: 4 (z_hi: 2, z_lo: 2; z = z_hi * 2 + z_lo), core: 2. Of those that a mesh axis runs over, the one named last changes fastest.
Arguments:
- adjoint_start: float32 [6, 16, 128, 1024], P(None, 'block', 'line'), may hold values from -6 to 6
- source: float32 [6, 16, 128, 1024], P(None, 'block', 'line'), may hold values from -6 to 6
- jacobian: float32 [6, 6, 16, 128, 1024], P(None, None, 'block', 'line'), may hold values from -0.45 to 3.6
- inv_diag: float32 [6, 6, 16, 128, 1024], P(None, None, 'block', 'line'), may hold values from -1 to 1
- lower_prop: float32 [6, 6, 16, 128, 1024], P(None, None, 'block', 'line'), may hold values from -1 to 1, as said below
- upper_prop: float32 [6, 6, 16, 128, 1024], P(None, None, 'block', 'line'), may hold values from -1 to 1, as said below
- send_cells: int32 [16, 8, 16, 512], P('block', 'line'), may hold values from -1 to 16383, as said below
- recv_cells: int32 [16, 8, 16, 512], P('block', 'line'), may hold values from -1 to 16383, as said below
- face_weight: float32 [16, 8, 16, 512], P('block', 'line'), may hold values from 0.2 to 0.6
- cycle_cells: int32 [16, 8, 512], P('block', 'line'), may hold values from 0 to 16383
- iface_cells: int32 [16, 8, 512], P('block', 'line'), may hold values from -1 to 16383, as said below
- iface_donor: int32 [16, 8, 2, 512], P('block', 'line'), may hold values from 0 to 8191, as said below
- iface_weight: float32 [16, 8, 2, 512], P('block', 'line'), may hold values from 0.1 to 0.5
Outputs:
- adjoint: float32 [6, 16, 128, 1024], P(None, 'block', 'line')
Inputs may be any that keep to these rules, and one draw needn't show every extreme that they name: For every source block p, destination block b and line group q, slot s of send_cells[p, q, b] is live (not -1) exactly when slot s of recv_cells[b, q, p] is; live slots come first; a block never faces itself, and every block receives 512 live slots from the next block (index b + 1 modulo 16). `recv_cells`: same liveness as send_cells; several slots may feed one cell. `iface_cells`: live slots come first; the devices of block 0 have all 512 slots live. `iface_donor`: the second donor of a slot is the first plus one. `lower_prop`: lower triangular in the variables. `upper_prop`: upper triangular in the variables.
All inputs are finite; a program needn't handle non-finite values.
Results may differ from a plain program's by a relative error of at most 0.0001.
Values sent between devices are 32-bit elements; how exact they have to be, the bound alone decides.
No kernel may reach another device: no remote copies, remote signals or barrier semaphores. Data moves between devices by JAX's collectives and lax.ppermute only.
A program may use at most 384 MiB of HBM per device.

v0:
```python
import jax
import jax.numpy as jnp
from jax import lax
from jax.experimental import pallas as pl
from jax.experimental.pallas import tpu as pltpu
from jax.sharding import PartitionSpec as P

NV = 6
KN = 16
NB = 16
NQ = 8
ITERS = 2
F32 = jnp.float32
BF16 = jnp.bfloat16
LOW = [(i, j) for i in range(NV) for j in range(i + 1)]
UPP = [(i, j) for i in range(NV) for j in range(i, NV)]
LOW_AT = {ij: n for n, ij in enumerate(LOW)}
UPP_AT = {ij: n for n, ij in enumerate(UPP)}
NP = len(LOW)
NH = NV * NV
NPHW = 2 * NP + NH

VMEM = pl.BlockSpec(memory_space=pltpu.VMEM)
ANY = pl.BlockSpec(memory_space=pl.ANY)
SMEM = pl.BlockSpec(memory_space=pltpu.SMEM)


def rows_of(x):
    n = x.size // (16 * 1024)
    x = x.reshape(n, 2, 8, 8, 128)
    return jnp.transpose(x, (0, 1, 3, 2, 4)).reshape(n * 128, 128)


def from_rows(x, n):
    x = x.reshape(n, 2, 8, 8, 128)
    return jnp.transpose(x, (0, 1, 3, 2, 4)).reshape(n, 16, 1024)


def at_k(ref, n, k):
    return ref[pl.ds(n * 128 + (k // 8) * 64 + k % 8, 8, stride=8), :]


def put_k(ref, n, k, value):
    ref[pl.ds(n * 128 + (k // 8) * 64 + k % 8, 8, stride=8), :] = value


def total(terms):
    terms = list(terms)
    while len(terms) > 1:
        nxt = [terms[i] + terms[i + 1] for i in range(0, len(terms) - 1, 2)]
        if len(terms) % 2:
            nxt.append(terms[-1])
        terms = nxt
    return terms[0]


def split_two(x):
    high = x.astype(BF16)
    low = (x - high.astype(F32)).astype(BF16)
    return high, low


def one_hot(index, count):
    rows = lax.broadcasted_iota(jnp.int32, (count, index.shape[1]), 0)
    return jnp.where(rows == index, 1.0, 0.0).astype(BF16)


def stage_table(table, x_ref, v, rows):
    t = table.T
    t = jnp.concatenate([t[:64], t[64:]], axis=1)
    high, low = split_two(t)
    x_ref[pl.ds(v * 64, 64), 0 : 2 * rows] = high
    x_ref[pl.ds(v * 64, 64), 2 * rows : 4 * rows] = low


def pick(x_ref, cell, rows):
    lane = jnp.bitwise_and(cell, 127)
    row = jnp.right_shift(cell, 7)
    key = jnp.right_shift(lane, 6) * rows + row
    low = jnp.bitwise_and(lane, 63)
    hot = one_hot(key, 2 * rows)
    hot = jnp.concatenate([hot, hot], axis=0)
    t = jnp.dot(x_ref[:, : 4 * rows], hot, preferred_element_type=F32)
    mask = lax.broadcasted_iota(jnp.int32, (64, cell.shape[1]), 0) == low
    return [
        jnp.sum(jnp.where(mask, t[v * 64 : (v + 1) * 64], 0.0), axis=0, keepdims=True) for v in range(NV)
    ]


def gather_all(cells_ref, send_ref, cycle_ref, out_ref, x_ref):
    for v in range(NV):
        stage_table(cells_ref[pl.ds(v * 128, 128), :], x_ref, v, 128)

    def face(p, carry):
        cell = jnp.maximum(send_ref[pl.ds(p, 1), :], 0)
        got = pick(x_ref, cell, 128)
        for v in range(NV):
            for c in range(4):
                out_ref[p, c * 12 + v : c * 12 + v + 1, :] = got[v][:, c * 128 : (c + 1) * 128]
        return carry

    lax.fori_loop(0, NB, face, 0)
    got = pick(x_ref, cycle_ref[...], 128)
    for v in range(NV):
        for c in range(4):
            r = c * 12 + 6 + v
            piece = jnp.broadcast_to(got[v][:, c * 128 : (c + 1) * 128][None], (NB, 1, 128))
            out_ref[:, r : r + 1, :] = piece


def first_gather_kernel(start_ref, send_ref, cycle_ref, out_ref, cells_ref, x_ref):
    for v in range(NV):
        for k in range(KN):
            cells_ref[pl.ds(v * 128 + k * 8, 8), :] = at_k(start_ref, v, k)
    gather_all(cells_ref, send_ref, cycle_ref, out_ref, x_ref)


def propagator_kernel(low_ref, upp_ref, out_ref, g_ref):
    def lower(k):
        return {ij: at_k(low_ref, ij[0] * NV + ij[1], k) for ij in LOW}

    def upper(k):
        return {ij: at_k(upp_ref, ij[0] * NV + ij[1], k) for ij in UPP}

    def g_at(k, ij):
        return pl.ds((k * NP + LOW_AT[ij]) * 8, 8)

    for j in range(NV):
        col = None
        for k in range(KN):
            if k == 0:
                col = {i: at_k(low_ref, i * NV + j, 0) for i in range(j, NV)}
            else:
                col = {
                    i: total(at_k(low_ref, i * NV + m, k) * col[m] for m in range(j, i + 1)) for i in range(j, NV)
                }
            for i in range(j, NV):
                g_ref[g_at(k, (i, j)), :] = col[i]
        for i in range(j, NV):
            out_ref[pl.ds(LOW_AT[(i, j)] * 8, 8), :] = col[i]

    for j in range(NV):
        hcol = {i: g_ref[g_at(KN - 1, (i, j)), :] for i in range(j, NV)}
        hcol.update({i: jnp.zeros((8, 128), F32) for i in range(j)})
        wcol = {i: at_k(upp_ref, i * NV + j, KN - 1) for i in range(j + 1)}
        for k in range(KN - 2, -1, -1):
            u = {(i, m): at_k(upp_ref, i * NV + m, k) for (i, m) in UPP}
            new_h = {}
            for i in range(NV):
                terms = [u[(i, m)] * hcol[m] for m in range(i, NV)]
                if i >= j:
                    terms.append(g_ref[g_at(k, (i, j)), :])
                new_h[i] = total(terms)
            wcol = {i: total(u[(i, m)] * wcol[m] for m in range(i, j + 1)) for i in range(j + 1)}
            hcol = new_h
        for i in range(NV):
            out_ref[pl.ds((NP + i * NV + j) * 8, 8), :] = hcol[i]
        for i in range(j + 1):
            out_ref[pl.ds((NP + NH + UPP_AT[(i, j)]) * 8, 8), :] = wcol[i]


def residual_kernel(
    recv_ref,
    recv_cells_ref,
    face_weight_ref,
    iface_cells_ref,
    donor_ref,
    iface_weight_ref,
    cells_ref,
    source_ref,
    jac_any,
    inv_any,
    low_any,
    upp_any,
    bound_ref,
    drive_ref,
    jac_ref,
    inv_ref,
    low_ref,
    upp_ref,
    acc_ref,
    x_ref,
    y_ref,
    sem,
):
    copies = [
        pltpu.make_async_copy(src, dst, sem.at[n])
        for n, (src, dst) in enumerate(
            [(jac_any, jac_ref), (inv_any, inv_ref), (low_any, low_ref), (upp_any, upp_ref)]
        )
    ]
    for copy in copies:
        copy.start()

    def add_slots(values, target):
        row = jnp.right_shift(target, 7)
        lane = jnp.bitwise_and(target, 127)
        hot_row = one_hot(jnp.bitwise_and(row, 63), 64)
        hot_lane = one_hot(jnp.right_shift(row, 6) * 128 + lane, 256)
        parts = []
        for v in range(NV):
            wide = jnp.broadcast_to(values[v], (16, values[v].shape[1]))
            parts.append(split_two(wide))
        left = jnp.concatenate(
            [hot_row * jnp.concatenate([parts[v][h]] * 4, axis=0) for h in range(2) for v in range(NV)], axis=0
        )
        acc_ref[...] += lax.dot_general(
            left, hot_lane, (((1,), (1,)), ((), ())), preferred_element_type=F32
        )

    acc_ref[...] = jnp.zeros_like(acc_ref)

    def face(p, carry):
        weight = face_weight_ref[pl.ds(p, 1), :]
        values = []
        for v in range(NV):
            got = jnp.concatenate(
                [recv_ref[pl.ds(p * 48 + c * 12 + v, 1), :] for c in range(4)], axis=1
            )
            values.append(got * weight)
        add_slots(values, recv_cells_ref[pl.ds(p, 1), :])
        return carry

    lax.fori_loop(0, NB, face, 0)

    for v in range(NV):
        stage_table(recv_ref[pl.ds(6 + v, 64, stride=12), :], x_ref, v, 64)
    first = pick(x_ref, donor_ref[0:1, :], 64)
    second = pick(x_ref, donor_ref[1:2, :], 64)
    w0 = iface_weight_ref[0:1, :]
    w1 = iface_weight_ref[1:2, :]
    add_slots([first[v] * w0 + second[v] * w1 for v in range(NV)], iface_cells_ref[...])

    for copy in copies:
        copy.wait()

    y = None
    for k in range(KN):
        a = [cells_ref[pl.ds(v * 128 + k * 8, 8), :] for v in range(NV)]
        r = []
        half, row = k // 8, (k % 8) * 8
        lanes = slice(half * 128, half * 128 + 128)
        for i in range(NV):
            coupled = acc_ref[i * 64 + row : i * 64 + row + 8, lanes]
            coupled = coupled + acc_ref[384 + i * 64 + row : 384 + i * 64 + row + 8, lanes]
            product = total(at_k(jac_ref, i * NV + j, k) * a[j] for j in range(NV))
            r.append(at_k(source_ref, i, k) - (product - coupled))
        d = [total(at_k(inv_ref, i * NV + j, k) * r[j] for j in range(NV)) for i in range(NV)]
        if k == 0:
            y = d
        else:
            y = [d[i] + total(at_k(low_ref, i * NV + j, k) * y[j] for j in range(i + 1)) for i in range(NV)]
        for i in range(NV):
            drive_ref[pl.ds(i * 128 + k * 8, 8), :] = d[i]
            y_ref[pl.ds(i * 128 + k * 8, 8), :] = y[i]
    u = y
    for k in range(KN - 2, -1, -1):
        u = [
            y_ref[pl.ds(i * 128 + k * 8, 8), :]
            + total(at_k(upp_ref, i * NV + j, k) * u[j] for j in range(i, NV))
            for i in range(NV)
        ]
    for i in range(NV):
        for q in range(NQ):
            bound_ref[q, pl.ds(i * 8, 8), :] = y[i]
            bound_ref[q, pl.ds(48 + i * 8, 8), :] = u[i]


def solve_lines(q_ref, bound_ref, phw_ref, drive_ref, low_ref, upp_ref, cells_ref, yin_ref, uin_ref, y_ref, put):
    zero = jnp.zeros((8, 128), F32)

    def p_at(p, i, j):
        return phw_ref[p, pl.ds(LOW_AT[(i, j)] * 8, 8), :]

    def h_at(p, i, j):
        return phw_ref[p, pl.ds((NP + i * NV + j) * 8, 8), :]

    def w_at(p, i, j):
        return phw_ref[p, pl.ds((NP + NH + UPP_AT[(i, j)]) * 8, 8), :]

    y = [zero] * NV
    for p in range(NQ):
        for i in range(NV):
            yin_ref[p, pl.ds(i * 8, 8), :] = y[i]
        if p + 1 < NQ:
            y = [
                bound_ref[p, pl.ds(i * 8, 8), :] + total(p_at(p, i, j) * y[j] for j in range(i + 1))
                for i in range(NV)
            ]
    u = [zero] * NV
    for p in range(NQ - 1, -1, -1):
        for i in range(NV):
            uin_ref[p, pl.ds(i * 8, 8), :] = u[i]
        if p > 0:
            yp = [yin_ref[p, pl.ds(i * 8, 8), :] for i in range(NV)]
            u = [
                bound_ref[p, pl.ds(48 + i * 8, 8), :]
                + total(h_at(p, i, j) * yp[j] for j in range(NV))
                + total(w_at(p, i, j) * u[j] for j in range(i, NV))
                for i in range(NV)
            ]
    q = q_ref[0]
    y = [yin_ref[q, pl.ds(i * 8, 8), :] for i in range(NV)]
    u = [uin_ref[q, pl.ds(i * 8, 8), :] for i in range(NV)]
    for k in range(KN):
        y = [
            drive_ref[pl.ds(i * 128 + k * 8, 8), :]
            + total(at_k(low_ref, i * NV + j, k) * y[j] for j in range(i + 1))
            for i in range(NV)
        ]
        for i in range(NV):
            y_ref[pl.ds(i * 128 + k * 8, 8), :] = y[i]
    for k in range(KN - 1, -1, -1):
        u = [
            y_ref[pl.ds(i * 128 + k * 8, 8), :]
            + total(at_k(upp_ref, i * NV + j, k) * u[j] for j in range(i, NV))
            for i in range(NV)
        ]
        for i in range(NV):
            put(i, k, cells_ref[pl.ds(i * 128 + k * 8, 8), :] + u[i])


def update_kernel(
    q_ref, bound_ref, phw_ref, drive_ref, low_ref, upp_ref, cells_ref, send_ref, cycle_ref,
    out_ref, new_ref, yin_ref, uin_ref, y_ref, x_ref,
):
    def put(i, k, value):
        new_ref[pl.ds(i * 128 + k * 8, 8), :] = value

    solve_lines(q_ref, bound_ref, phw_ref, drive_ref, low_ref, upp_ref, cells_ref, yin_ref, uin_ref, y_ref, put)
    gather_all(new_ref, send_ref, cycle_ref, out_ref, x_ref)


def final_kernel(
    q_ref, bound_ref, phw_ref, drive_ref, low_ref, upp_ref, cells_ref, new_ref, yin_ref, uin_ref, y_ref
):
    def put(i, k, value):
        put_k(new_ref, i, k, value)

    solve_lines(q_ref, bound_ref, phw_ref, drive_ref, low_ref, upp_ref, cells_ref, yin_ref, uin_ref, y_ref, put)


def f32(*shape):
    return jax.ShapeDtypeStruct(shape, F32)


PARAMS = pltpu.CompilerParams(vmem_limit_bytes=40 * 1024 * 1024)


def body(
    adjoint_start, source, jacobian, inv_diag, lower_prop, upper_prop, send_cells, recv_cells,
    face_weight, cycle_cells, iface_cells, iface_donor, iface_weight,
):
    start = rows_of(adjoint_start)
    src = rows_of(source)
    jac = rows_of(jacobian)
    inv = rows_of(inv_diag)
    low = rows_of(lower_prop)
    upp = rows_of(upper_prop)
    send = send_cells.reshape(NB, 512)
    recv_at = recv_cells.reshape(NB, 512)
    weight = face_weight.reshape(NB, 512)
    cycle = cycle_cells.reshape(1, 512)
    iface_at = iface_cells.reshape(1, 512)
    donor = iface_donor.reshape(2, 512)
    iface_w = iface_weight.reshape(2, 512)
    q = lax.axis_index("line").reshape(1).astype(jnp.int32)

    phw = pl.pallas_call(
        propagator_kernel,
        out_shape=f32(NPHW * 8, 128),
        in_specs=[VMEM] * 2,
        out_specs=VMEM,
        scratch_shapes=[pltpu.VMEM((KN * NP * 8, 128), F32)],
        compiler_params=PARAMS,
        name="propagators",
    )(low, upp)
    phw_all = lax.all_gather(phw, "line", axis=0)

    outgoing, cells = pl.pallas_call(
        first_gather_kernel,
        out_shape=(f32(NB, 48, 128), f32(NV * 128, 128)),
        in_specs=[VMEM] * 3,
        out_specs=(VMEM, VMEM),
        scratch_shapes=[pltpu.VMEM((384, 512), BF16)],
        compiler_params=PARAMS,
        name="first_gather",
    )(start, send, cycle)

    mats = [pltpu.VMEM((NV * NV * 128, 128), F32)] * 4
    line_scratch = [
        pltpu.VMEM((NQ, 48, 128), F32),
        pltpu.VMEM((NQ, 48, 128), F32),
        pltpu.VMEM((NV * 128, 128), F32),
    ]
    for iteration in range(ITERS):
        incoming = lax.all_to_all(outgoing, "block", split_axis=0, concat_axis=0, tiled=True)
        bound, drive = pl.pallas_call(
            residual_kernel,
            out_shape=(f32(NQ, 96, 128), f32(NV * 128, 128)),
            in_specs=[VMEM] * 8 + [ANY] * 4,
            out_specs=(VMEM, VMEM),
            scratch_shapes=mats
            + [
                pltpu.VMEM((768, 256), F32),
                pltpu.VMEM((384, 256), BF16),
                pltpu.VMEM((NV * 128, 128), F32),
                pltpu.SemaphoreType.DMA((4,)),
            ],
            compiler_params=PARAMS,
            name="residual",
        )(incoming.reshape(NB * 48, 128), recv_at, weight, iface_at, donor, iface_w, cells, src, jac, inv, low, upp)
        bound_all = lax.all_to_all(bound, "line", split_axis=0, concat_axis=0, tiled=True)
        if iteration + 1 < ITERS:
            outgoing, cells = pl.pallas_call(
                update_kernel,
                out_shape=(f32(NB, 48, 128), f32(NV * 128, 128)),
                in_specs=[SMEM] + [VMEM] * 8,
                out_specs=(VMEM, VMEM),
                scratch_shapes=line_scratch + [pltpu.VMEM((384, 512), BF16)],
                compiler_params=PARAMS,
                name="update",
            )(q, bound_all, phw_all, drive, low, upp, cells, send, cycle)
        else:
            result = pl.pallas_call(
                final_kernel,
                out_shape=f32(NV * 128, 128),
                in_specs=[SMEM] + [VMEM] * 6,
                out_specs=VMEM,
                scratch_shapes=line_scratch,
                compiler_params=PARAMS,
                name="final_update",
            )(q, bound_all, phw_all, drive, low, upp, cells)
    return from_rows(result, NV)[:, None]


def solution(mesh):
    cell = P(None, "block", "line", None)
    matrix = P(None, None, "block", "line", None)
    slots = P("block", "line", None, None)
    flat = P("block", "line", None)
    placed = (cell, cell, matrix, matrix, matrix, matrix, slots, slots, slots, flat, flat, slots, slots)
    return jax.shard_map(body, mesh=mesh, in_specs=placed, out_specs=cell, check_vma=False)
```

profile of v0, /device:TPU:0, one launch (start us, length us, event | category | flops | bytes accessed | tf_op | source)
XLA Modules:
  0.0 139.5 jit_solution(9749331239082401787)
XLA Ops:
  6.5 0.0 all-gather.3.cloned.1.call-start
  6.5 0.0 copy-start
  6.5 1.7 %copy-done = f32[6,6,1,16,1024]{4,3,2,1,0:T(8,128)S(1)} copy-done((f32[6,6,1,16,1024]{4,3,2,1,0:T(8,128)S(1)}, f32[6,6,1,16,1024]{4,3,2,1,0:T(8,128)}, u32[]{:S(2)}) %copy-start) | copy-done | bytes 2359320
  8.2 0.0 copy-start.2
  8.2 1.7 %copy-done.2 = f32[6,6,1,16,1024]{4,3,2,1,0:T(8,128)S(1)} copy-done((f32[6,6,1,16,1024]{4,3,2,1,0:T(8,128)S(1)}, f32[6,6,1,16,1024]{4,3,2,1,0:T(8,128)}, u32[]{:S(2)}) %copy-start.2) | copy-done | bytes 2359320
  9.9 0.0 copy-start.16
  9.9 0.0 copy-start.25
  9.9 0.0 copy-start.1
  9.9 0.0 copy-start.12
  9.9 0.0 copy-start.23
  9.9 0.0 copy-start.24
  9.9 0.0 copy-start.26
  9.9 3.0 %propagators.1 = f32[624,128]{1,0:T(8,128)} custom-call(f32[4608,128]{1,0:T(8,128)S(1)} %bitcast.46, f32[4608,128]{1,0:T(8,128)S(1)} %bitcast.51), custom_call_target="tpu_custom_call" | custom-call | tf_op jit(solution)/shard_map/propagators/pallas_call | solution.py:369
  12.9 0.0 all-gather.3.cloned.1.call-update
  12.9 0.0 copy-done.16
  12.9 0.0 copy-done.25
  12.9 0.0 copy-start.21
  12.9 0.7 copy-done.21
  13.7 7.1 %first_gather.1 = (f32[16,48,128]{2,1,0:T(8,128)S(1)}, f32[768,128]{1,0:T(8,128)S(1)}) custom-call(f32[768,128]{1,0:T(8,128)S(1)} %bitcast.66, s32[16,512]{1,0:T(8,128)S(1)} %bitcast.71, s32[1,512]{1,0:T(1,128)S(1)} %bitcast.77), custom_call_target="tpu_custom_call" | custom-call | tf_op jit(solution)/shard_map/first_gather/pallas_call | solution.py:380
  20.8 26.0 %all_to_all.20 = f32[16,48,128]{2,1,0:T(8,128)S(1)} all-to-all(f32[16,48,128]{2,1,0:T(8,128)S(1)} %get-tuple-element.13), channel_id=1, replica_groups=mesh['block'=16,'line'=8] {'block'}, dimensions={0} | all-to-all | bytes 786432 | tf_op jit(solution)/shard_map/all_to_all | solution.py:397
  46.8 0.0 copy-done.1
  46.8 0.0 copy-done.12
  46.8 0.0 copy-done.23
  46.8 0.0 copy-done.24
  46.9 0.0 copy-done.26
  46.9 0.0 copy-start.3
  46.9 1.7 %copy-done.3 = f32[6,6,1,16,1024]{4,3,2,1,0:T(8,128)S(1)} copy-done((f32[6,6,1,16,1024]{4,3,2,1,0:T(8,128)S(1)}, f32[6,6,1,16,1024]{4,3,2,1,0:T(8,128)}, u32[]{:S(2)}) %copy-start.3) | copy-done | bytes 2359320
  48.6 0.0 copy-start.8
  48.6 1.7 %copy-done.8 = f32[6,6,1,16,1024]{4,3,2,1,0:T(8,128)S(1)} copy-done((f32[6,6,1,16,1024]{4,3,2,1,0:T(8,128)S(1)}, f32[6,6,1,16,1024]{4,3,2,1,0:T(8,128)}, u32[]{:S(2)}) %copy-start.8) | copy-done | bytes 2359320
  50.2 0.0 copy-start.10
  50.2 1.7 %copy-done.10 = f32[6,6,1,16,1024]{4,3,2,1,0:T(8,128)S(1)} copy-done((f32[6,6,1,16,1024]{4,3,2,1,0:T(8,128)S(1)}, f32[6,6,1,16,1024]{4,3,2,1,0:T(8,128)}, u32[]{:S(2)}) %copy-start.10) | copy-done | bytes 2359320
  51.9 0.0 copy-start.17
  51.9 0.8 copy-done.17
  52.7 0.0 copy-start.19
  52.7 0.8 copy-done.19
  53.5 10.4 %residual.2 = (f32[8,96,128]{2,1,0:T(8,128)S(1)}, f32[768,128]{1,0:T(8,128)S(1)}) custom-call(f32[768,128]{1,0:T(8,128)S(1)} %bitcast.64, s32[16,512]{1,0:T(8,128)S(1)} %bitcast.67, f32[16,512]{1,0:T(8,128)S(1)} %bitcast.69, s32[1,512]{1,0:T(1,128)S(1)} %bitcast.79, s32[2,512]{1,0:T(2,128)S(1)} %bitcast.73, f32[2,512]{1,0:T(2,128)S(1)} %bitcast.75, ...), custom_call_target="tpu_custom_call" | custom-call | tf_op jit(solution)/shard_map/residual/pallas_call | solution.py:398
  63.8 0.0 copy-start.13
  63.9 0.7 copy-done.13
  64.6 0.0 copy-start.15
  64.6 0.7 copy-done.15
  65.3 8.5 %all-to-all-start.1 = ((f32[8,96,128]{2,1,0:T(8,128)}), f32[8,96,128]{2,1,0:T(8,128)S(1)}, u32[]{:S(2)}, u32[]{:S(2)}) async-start(f32[8,96,128]{2,1,0:T(8,128)} %copy-done.15), calls=%async_computation.1 | async-start | bytes 786432 | tf_op jit(solution)/shard_map/all_to_all | solution.py:413
  73.9 9.5 %all-to-all-done.1.bound_ref = f32[8,96,128]{2,1,0:T(8,128)S(1)} async-done(((f32[8,96,128]{2,1,0:T(8,128)}), f32[8,96,128]{2,1,0:T(8,128)S(1)}, u32[]{:S(2)}, u32[]{:S(2)}) %all-to-all-start.1) | async-done | bytes 393248 | tf_op jit(solution)/shard_map/all_to_all | solution.py:413
  83.4 0.0 all-gather.3.cloned.1.call-done
  83.4 0.0 copy-start.4
  83.4 1.7 %copy-done.4 = f32[6,6,1,16,1024]{4,3,2,1,0:T(8,128)S(1)} copy-done((f32[6,6,1,16,1024]{4,3,2,1,0:T(8,128)S(1)}, f32[6,6,1,16,1024]{4,3,2,1,0:T(8,128)}, u32[]{:S(2)}) %copy-start.4) | copy-done | bytes 2359320
  85.1 0.0 copy-start.6
  85.1 1.7 %copy-done.6 = f32[4992,128]{1,0:T(8,128)S(1)} copy-done((f32[4992,128]{1,0:T(8,128)S(1)}, f32[4992,128]{1,0:T(8,128)}, u32[]{:S(2)}) %copy-start.6) | copy-done | bytes 2555928
  86.8 0.0 copy-start.14
  86.8 1.0 copy-done.14
  87.8 0.0 copy-start.22
  87.8 0.8 copy-done.22
  88.5 0.0 copy-start.20
  88.6 7.8 %update.1 = (f32[16,48,128]{2,1,0:T(8,128)S(1)}, f32[768,128]{1,0:T(8,128)S(1)}) custom-call(s32[1]{0:T(128)} %bitcast.q_ref, f32[8,96,128]{2,1,0:T(8,128)S(1)} %all-to-all-done.1.bound_ref, f32[8,624,128]{2,1,0:T(8,128)S(1)} %bitcast.56, f32[768,128]{1,0:T(8,128)S(1)} %copy-done.14, f32[4608,128]{1,0:T(8,128)S(1)} %bitcast.48, f32[4608,128]{1,0:T(8,128)S(1)} %bitcast.53, ...), custom_call_target="tpu_custom_call" | custom-call | tf_op jit(solution)/shard_map/update/pallas_call | solution.py:415
  96.4 13.3 %all_to_all.21 = f32[16,48,128]{2,1,0:T(8,128)S(1)} all-to-all(f32[16,48,128]{2,1,0:T(8,128)S(1)} %get-tuple-element.17), channel_id=1, replica_groups=mesh['block'=16,'line'=8] {'block'}, dimensions={0} | all-to-all | bytes 786432 | tf_op jit(solution)/shard_map/all_to_all | solution.py:397
  109.7 0.0 copy-done.5
  109.7 0.0 copy-done.9
  109.7 0.0 copy-done.11
  109.7 0.0 copy-done.18
  109.7 0.0 copy-done.20
  109.7 0.0 copy-start.7
  109.7 10.4 %residual.3 = (f32[8,96,128]{2,1,0:T(8,128)S(1)}, f32[768,128]{1,0:T(8,128)S(1)}) custom-call(f32[768,128]{1,0:T(8,128)S(1)} %bitcast.65, s32[16,512]{1,0:T(8,128)S(1)} %bitcast.68, f32[16,512]{1,0:T(8,128)S(1)} %bitcast.70, s32[1,512]{1,0:T(1,128)S(1)} %bitcast.80, s32[2,512]{1,0:T(2,128)S(1)} %bitcast.74, f32[2,512]{1,0:T(2,128)S(1)} %bitcast.76, ...), custom_call_target="tpu_custom_call" | custom-call | tf_op jit(solution)/shard_map/residual/pallas_call | solution.py:398
  120.2 11.0 %all_to_all.22.bound_ref = f32[8,96,128]{2,1,0:T(8,128)S(1)} all-to-all(f32[8,96,128]{2,1,0:T(8,128)S(1)} %get-tuple-element.19), channel_id=1, replica_groups=mesh['block'=16,'line'=8] {'line'}, dimensions={0} | all-to-all | bytes 786432 | tf_op jit(solution)/shard_map/all_to_all | solution.py:413
  131.1 0.0 copy-done.7
  131.1 1.5 %final_update.1 = f32[768,128]{1,0:T(8,128)} custom-call(s32[1]{0:T(128)} %bitcast.q_ref, f32[8,96,128]{2,1,0:T(8,128)S(1)} %all_to_all.22.bound_ref, f32[8,624,128]{2,1,0:T(8,128)S(1)} %bitcast.57, f32[768,128]{1,0:T(8,128)S(1)} %get-tuple-element.20.drive_ref, f32[4608,128]{1,0:T(8,128)S(1)} %bitcast.50, f32[4608,128]{1,0:T(8,128)S(1)} %bitcast.55, ...), custom_call_target="tpu_custom_call" | custom-call | tf_op jit(solution)/shard_map/final_update/pallas_call | solution.py:425
  (4 shorter events, 0.0 us)
Async XLA Ops:
  6.5 76.9 %all-gather.3.cloned.1.call-start = ((), (), s32[]{:S(2)}) async-start(), calls=%async_computation.4 | async-start | bytes 2875392 | tf_op jit(solution)/shard_map/all_gather | solution.py:378
  6.5 1.7 %copy-start = (f32[6,6,1,16,1024]{4,3,2,1,0:T(8,128)S(1)}, f32[6,6,1,16,1024]{4,3,2,1,0:T(8,128)}, u32[]{:S(2)}) copy-start(f32[6,6,1,16,1024]{4,3,2,1,0:T(8,128)} %param.17) | copy-start | bytes 7077892
  8.2 1.7 %copy-start.2 = (f32[6,6,1,16,1024]{4,3,2,1,0:T(8,128)S(1)}, f32[6,6,1,16,1024]{4,3,2,1,0:T(8,128)}, u32[]{:S(2)}) copy-start(f32[6,6,1,16,1024]{4,3,2,1,0:T(8,128)} %param.18) | copy-start | bytes 7077892
  9.9 3.0 %copy-start.16 = (f32[6,1,16,1024]{3,2,1,0:T(8,128)S(1)}, f32[6,1,16,1024]{3,2,1,0:T(8,128)}, u32[]{:S(2)}) copy-start(f32[6,1,16,1024]{3,2,1,0:T(8,128)} %param.13) | copy-start | bytes 1179652
  9.9 3.0 %copy-start.25 = (s32[1,1,512]{2,1,0:T(1,128)S(1)}, s32[1,1,512]{2,1,0:T(1,128)}, u32[]{:S(2)}) copy-start(s32[1,1,512]{2,1,0:T(1,128)} %param.22) | copy-start | bytes 6148
  9.9 37.0 %copy-start.1 = (f32[6,6,1,16,1024]{4,3,2,1,0:T(8,128)S(1)}, f32[6,6,1,16,1024]{4,3,2,1,0:T(8,128)}, u32[]{:S(2)}) copy-start(f32[6,6,1,16,1024]{4,3,2,1,0:T(8,128)} %param.17) | copy-start | bytes 7077892
  9.9 37.0 %copy-start.12 = (f32[6,1,16,1024]{3,2,1,0:T(8,128)S(1)}, f32[6,1,16,1024]{3,2,1,0:T(8,128)}, u32[]{:S(2)}) copy-start(f32[6,1,16,1024]{3,2,1,0:T(8,128)} %param.14) | copy-start | bytes 1179652
  9.9 37.0 %copy-start.23 = (s32[1,1,2,512]{3,2,1,0:T(2,128)S(1)}, s32[1,1,2,512]{3,2,1,0:T(2,128)}, u32[]{:S(2)}) copy-start(s32[1,1,2,512]{3,2,1,0:T(2,128)} %param.24) | copy-start | bytes 12292
  9.9 37.0 %copy-start.24 = (f32[1,1,2,512]{3,2,1,0:T(2,128)S(1)}, f32[1,1,2,512]{3,2,1,0:T(2,128)}, u32[]{:S(2)}) copy-start(f32[1,1,2,512]{3,2,1,0:T(2,128)} %param.25) | copy-start | bytes 12292
  9.9 37.0 %copy-start.26 = (s32[1,1,512]{2,1,0:T(1,128)S(1)}, s32[1,1,512]{2,1,0:T(1,128)}, u32[]{:S(2)}) copy-start(s32[1,1,512]{2,1,0:T(1,128)} %param.23) | copy-start | bytes 6148
  12.9 0.8 copy-start.21
  46.9 1.7 %copy-start.3 = (f32[6,6,1,16,1024]{4,3,2,1,0:T(8,128)S(1)}, f32[6,6,1,16,1024]{4,3,2,1,0:T(8,128)}, u32[]{:S(2)}) copy-start(f32[6,6,1,16,1024]{4,3,2,1,0:T(8,128)} %param.18) | copy-start | bytes 7077892
  48.6 1.7 %copy-start.8 = (f32[6,6,1,16,1024]{4,3,2,1,0:T(8,128)S(1)}, f32[6,6,1,16,1024]{4,3,2,1,0:T(8,128)}, u32[]{:S(2)}) copy-start(f32[6,6,1,16,1024]{4,3,2,1,0:T(8,128)} %param.15) | copy-start | bytes 7077892
  50.2 1.7 %copy-start.10 = (f32[6,6,1,16,1024]{4,3,2,1,0:T(8,128)S(1)}, f32[6,6,1,16,1024]{4,3,2,1,0:T(8,128)}, u32[]{:S(2)}) copy-start(f32[6,6,1,16,1024]{4,3,2,1,0:T(8,128)} %param.16) | copy-start | bytes 7077892
  51.9 0.8 copy-start.17
  52.7 0.8 copy-start.19
  63.8 0.7 copy-start.13
  64.6 0.7 copy-start.15
  65.3 18.0 %all-to-all-start.1 = ((f32[8,96,128]{2,1,0:T(8,128)}), f32[8,96,128]{2,1,0:T(8,128)S(1)}, u32[]{:S(2)}, u32[]{:S(2)}) async-start(f32[8,96,128]{2,1,0:T(8,128)} %copy-done.15), calls=%async_computation.1 | async-start | bytes 786432 | tf_op jit(solution)/shard_map/all_to_all | solution.py:413
  83.4 1.7 %copy-start.4 = (f32[6,6,1,16,1024]{4,3,2,1,0:T(8,128)S(1)}, f32[6,6,1,16,1024]{4,3,2,1,0:T(8,128)}, u32[]{:S(2)}) copy-start(f32[6,6,1,16,1024]{4,3,2,1,0:T(8,128)} %param.18) | copy-start | bytes 7077892
  85.1 1.7 %copy-start.6 = (f32[4992,128]{1,0:T(8,128)S(1)}, f32[4992,128]{1,0:T(8,128)}, u32[]{:S(2)}) copy-start(f32[4992,128]{1,0:T(8,128)} %all-gather.3.cloned.1.call-done) | copy-start | bytes 7667716
  86.8 1.0 copy-start.14
  87.8 0.8 copy-start.22
  88.5 21.2 %copy-start.5 = (f32[6,6,1,16,1024]{4,3,2,1,0:T(8,128)S(1)}, f32[6,6,1,16,1024]{4,3,2,1,0:T(8,128)}, u32[]{:S(2)}) copy-start(f32[6,6,1,16,1024]{4,3,2,1,0:T(8,128)} %param.18) | copy-start | bytes 7077892
  88.5 21.2 %copy-start.9 = (f32[6,6,1,16,1024]{4,3,2,1,0:T(8,128)S(1)}, f32[6,6,1,16,1024]{4,3,2,1,0:T(8,128)}, u32[]{:S(2)}) copy-start(f32[6,6,1,16,1024]{4,3,2,1,0:T(8,128)} %param.15) | copy-start | bytes 7077892
  88.5 21.2 %copy-start.11 = (f32[6,6,1,16,1024]{4,3,2,1,0:T(8,128)S(1)}, f32[6,6,1,16,1024]{4,3,2,1,0:T(8,128)}, u32[]{:S(2)}) copy-start(f32[6,6,1,16,1024]{4,3,2,1,0:T(8,128)} %param.16) | copy-start | bytes 7077892
  88.5 21.2 %copy-start.18 = (s32[1,1,16,512]{3,2,1,0:T(8,128)S(1)}, s32[1,1,16,512]{3,2,1,0:T(8,128)}, u32[]{:S(2)}) copy-start(s32[1,1,16,512]{3,2,1,0:T(8,128)} %param.20) | copy-start | bytes 98308
  88.5 21.2 %copy-start.20 = (f32[1,1,16,512]{3,2,1,0:T(8,128)S(1)}, f32[1,1,16,512]{3,2,1,0:T(8,128)}, u32[]{:S(2)}) copy-start(f32[1,1,16,512]{3,2,1,0:T(8,128)} %param.21) | copy-start | bytes 98308
  109.7 21.4 %copy-start.7 = (f32[4992,128]{1,0:T(8,128)S(1)}, f32[4992,128]{1,0:T(8,128)}, u32[]{:S(2)}) copy-start(f32[4992,128]{1,0:T(8,128)} %all-gather.3.cloned.1.call-done) | copy-start | bytes 7667716
Sparse Core Ops, SparseCore 0:
  13.0 46.8 all-gather.2
where the time goes:
time: 140 us
  blocking collectives  50.4 us (36%)
  Pallas kernels  40.2 us (29%)
  local copies, waits for them, and re-layouts  17.3 us (12%)
  between operations  13.6 us (10%)
  waiting for transfers between devices  9.53 us (7%)
  starting transfers between devices  8.53 us (6%)
    all_to_all x2, blocking collectives, body(): lax.all_to_all(outgoing, 'block', split_axis=0, concat_axis=0, tiled=True)  39.4 us
    pallas_call x2, Pallas kernels, body(): pl.pallas_call(residual_kernel, out_shape=(f32(NQ, 96, 128), f32(NV * 128...  20.8 us
    unnamed x54, local copies, waits for them, and re-layouts  17.3 us
    all_to_all x1, blocking collectives, body(): lax.all_to_all(bound, 'line', split_axis=0, concat_axis=0, tiled=True)  11 us
    all_to_all x1, waiting for transfers between devices, body(): lax.all_to_all(bound, 'line', split_axis=0, concat_axis=0, tiled=True)  9.52 us
    all_to_all x1, starting transfers between devices, body(): lax.all_to_all(bound, 'line', split_axis=0, concat_axis=0, tiled=True)  8.53 us
    pallas_call x1, Pallas kernels, body(): pl.pallas_call(update_kernel, out_shape=(f32(NB, 48, 128), f32(NV * 128,...  7.79 us
    pallas_call x1, Pallas kernels, body(): pl.pallas_call(first_gather_kernel, out_shape=(f32(NB, 48, 128), f32(NV *...  7.11 us
  transfers between devices with their start and end apart: 2, of which 1 were waited for; matrix products, arithmetic and copies ran while one was open for 0% of the time, Pallas kernels for 13%

commit v1 on v0

v1 whole, which is shorter than its diff:
```python
from functools import partial

import jax
import jax.numpy as jnp
from jax import lax
from jax.experimental import pallas as pl
from jax.experimental.pallas import tpu as pltpu
from jax.sharding import PartitionSpec as P

NV = 6
KN = 16
NB = 16
NQ = 8
ITERS = 2
ORDER = True
PICK = 2 * 768 * 256 * 17 * 512
F32 = jnp.float32
BF16 = jnp.bfloat16
LOW = [(i, j) for i in range(NV) for j in range(i + 1)]
UPP = [(i, j) for i in range(NV) for j in range(i, NV)]
LOW_AT = {ij: n for n, ij in enumerate(LOW)}
UPP_AT = {ij: n for n, ij in enumerate(UPP)}
NP = len(LOW)
NH = NV * NV
NPHW = 2 * NP + NH
ROWS = 80
ENDS = 16
BOTH = ROWS + ENDS

VMEM = pl.BlockSpec(memory_space=pltpu.VMEM)
HBM = pl.BlockSpec(memory_space=pltpu.HBM)
SMEM = pl.BlockSpec(memory_space=pltpu.SMEM)


def rows_of(x):
    n = x.size // (16 * 1024)
    x = x.reshape(n, 2, 8, 8, 128)
    return jnp.transpose(x, (0, 1, 3, 2, 4)).reshape(n * 128, 128)


def from_rows(x, n):
    x = x.reshape(n, 2, 8, 8, 128)
    return jnp.transpose(x, (0, 1, 3, 2, 4)).reshape(n, 16, 1024)


def at_k(ref, n, k):
    return ref[pl.ds(n * 128 + (k // 8) * 64 + k % 8, 8, stride=8), :]


def put_k(ref, n, k, value):
    ref[pl.ds(n * 128 + (k // 8) * 64 + k % 8, 8, stride=8), :] = value


def total(terms):
    terms = list(terms)
    while len(terms) > 1:
        nxt = [terms[i] + terms[i + 1] for i in range(0, len(terms) - 1, 2)]
        if len(terms) % 2:
            nxt.append(terms[-1])
        terms = nxt
    return terms[0]


def split_two(x):
    high = x.astype(BF16)
    low = (x - high.astype(F32)).astype(BF16)
    return high, low


def one_hot(index, count):
    rows = lax.broadcasted_iota(jnp.int32, (count, index.shape[1]), 0)
    return jnp.where(rows == index, 1.0, 0.0).astype(BF16)


def stage_table(table, x_ref, v, rows):
    t = table.T
    t = jnp.concatenate([t[:64], t[64:]], axis=1)
    high, low = split_two(t)
    x_ref[v * 64 : v * 64 + 64, 0 : 2 * rows] = high
    x_ref[384 + v * 64 : 384 + v * 64 + 64, 0 : 2 * rows] = low


def pick(x_ref, cell, rows):
    lane = jnp.bitwise_and(cell, 127)
    row = jnp.right_shift(cell, 7)
    key = jnp.right_shift(lane, 6) * rows + row
    low = jnp.bitwise_and(lane, 63)
    t = jnp.dot(x_ref[:, : 2 * rows], one_hot(key, 2 * rows), preferred_element_type=F32)
    t = t[:384] + t[384:]
    mask = lax.broadcasted_iota(jnp.int32, (64, cell.shape[1]), 0) == low
    return [
        jnp.sum(jnp.where(mask, t[v * 64 : (v + 1) * 64], 0.0), axis=0, keepdims=True) for v in range(NV)
    ]


def gather_all(cells_ref, send_ref, cycle_ref, out_ref, x_ref):
    for v in range(NV):
        stage_table(cells_ref[pl.ds(v * 128, 128), :], x_ref, v, 128)
    for p in range(NB):
        got = pick(x_ref, jnp.maximum(send_ref[p : p + 1, :], 0), 128)
        for v in range(NV):
            for c in range(4):
                out_ref[p, c * 12 + v : c * 12 + v + 1, :] = got[v][:, c * 128 : (c + 1) * 128]
    got = pick(x_ref, cycle_ref[...], 128)
    for v in range(NV):
        for c in range(4):
            r = c * 12 + 6 + v
            piece = jnp.broadcast_to(got[v][:, c * 128 : (c + 1) * 128][None], (NB, 1, 128))
            out_ref[:, r : r + 1, :] = piece


def first_gather_kernel(start_ref, send_ref, cycle_ref, out_ref, cells_ref, x_ref):
    for v in range(NV):
        for k in range(KN):
            cells_ref[pl.ds((v * KN + k) * 8, 8), :] = at_k(start_ref, v, k)
    gather_all(cells_ref, send_ref, cycle_ref, out_ref, x_ref)


def prepare_kernel(low_ref, upp_ref, out_ref, lowc_ref, uppc_ref, g_ref):
    for i, j in LOW:
        for k in range(KN):
            lowc_ref[pl.ds((LOW_AT[(i, j)] * KN + k) * 8, 8), :] = at_k(low_ref, i * NV + j, k)
    for i, j in UPP:
        for k in range(KN):
            uppc_ref[pl.ds((UPP_AT[(i, j)] * KN + k) * 8, 8), :] = at_k(upp_ref, i * NV + j, k)

    def low(k, i, j):
        return lowc_ref[pl.ds((LOW_AT[(i, j)] * KN + k) * 8, 8), :]

    def upp(k, i, j):
        return uppc_ref[pl.ds((UPP_AT[(i, j)] * KN + k) * 8, 8), :]

    def g_at(k, i, j):
        return pl.ds((k * NP + LOW_AT[(i, j)]) * 8, 8)

    def send(n, value):
        out_ref[pl.ds(n, NQ, stride=ROWS), :] = value

    for j in range(NV):
        col = {i: low(0, i, j) for i in range(j, NV)}
        for i in range(j, NV):
            g_ref[g_at(0, i, j), :] = col[i]
        for k in range(1, KN):
            col = {i: total(low(k, i, m) * col[m] for m in range(j, i + 1)) for i in range(j, NV)}
            for i in range(j, NV):
                g_ref[g_at(k, i, j), :] = col[i]
        for i in range(j, NV):
            send(LOW_AT[(i, j)], col[i])

    for j in range(NV):
        hcol = {i: g_ref[g_at(KN - 1, i, j), :] if i >= j else jnp.zeros((8, 128), F32) for i in range(NV)}
        wcol = {i: upp(KN - 1, i, j) for i in range(j + 1)}
        for k in range(KN - 2, -1, -1):
            u = {(i, m): upp(k, i, m) for (i, m) in UPP}
            wcol = {i: total(u[(i, m)] * wcol[m] for m in range(i, j + 1)) for i in range(j + 1)}
            new_h = {}
            for i in range(NV):
                terms = [u[(i, m)] * hcol[m] for m in range(i, NV)]
                if i >= j:
                    terms.append(g_ref[g_at(k, i, j), :])
                new_h[i] = total(terms)
            hcol = new_h
        for i in range(NV):
            send(NP + i * NV + j, hcol[i])
        for i in range(j + 1):
            send(NP + NH + UPP_AT[(i, j)], wcol[i])


def residual_kernel(
    with_products,
    recv_ref,
    recv_cells_ref,
    face_weight_ref,
    iface_cells_ref,
    donor_ref,
    iface_weight_ref,
    cells_ref,
    source_ref,
    low_ref,
    upp_ref,
    jac_ref,
    inv_ref,
    *refs,
):
    if with_products:
        products_ref, *refs = refs
    bound_ref, drive_ref, acc_ref, x_ref, y_ref = refs
    stride = BOTH if with_products else ENDS
    if with_products:
        for q in range(NQ):
            bound_ref[q * BOTH : q * BOTH + ROWS, :] = products_ref[q * ROWS : (q + 1) * ROWS, :]
    def add_slots(values, target):
        row = jnp.right_shift(target, 7)
        lane = jnp.bitwise_and(target, 127)
        hot_row = one_hot(jnp.bitwise_and(row, 63), 64)
        hot_lane = one_hot(jnp.right_shift(row, 6) * 128 + lane, 256)
        parts = []
        for v in range(NV):
            wide = jnp.broadcast_to(values[v], (16, values[v].shape[1]))
            parts.append(split_two(wide))
        left = jnp.concatenate(
            [hot_row * jnp.concatenate([parts[v][h]] * 4, axis=0) for h in range(2) for v in range(NV)], axis=0
        )
        acc_ref[...] += lax.dot_general(
            left, hot_lane, (((1,), (1,)), ((), ())), preferred_element_type=F32
        )

    acc_ref[...] = jnp.zeros_like(acc_ref)
    for p in range(NB):
        weight = face_weight_ref[p : p + 1, :]
        values = []
        for v in range(NV):
            rows = [p * 48 + c * 12 + v for c in range(4)]
            values.append(jnp.concatenate([recv_ref[r : r + 1, :] for r in rows], axis=1) * weight)
        add_slots(values, recv_cells_ref[p : p + 1, :])

    for v in range(NV):
        stage_table(recv_ref[pl.ds(6 + v, 64, stride=12), :], x_ref, v, 64)
    first = pick(x_ref, donor_ref[0:1, :], 64)
    second = pick(x_ref, donor_ref[1:2, :], 64)
    w0 = iface_weight_ref[0:1, :]
    w1 = iface_weight_ref[1:2, :]
    add_slots([first[v] * w0 + second[v] * w1 for v in range(NV)], iface_cells_ref[...])

    y = None
    for k in range(KN):
        a = [cells_ref[pl.ds(v * 128 + k * 8, 8), :] for v in range(NV)]
        r = []
        half, row = k // 8, (k % 8) * 8
        lanes = slice(half * 128, half * 128 + 128)
        for i in range(NV):
            coupled = acc_ref[i * 64 + row : i * 64 + row + 8, lanes]
            coupled = coupled + acc_ref[384 + i * 64 + row : 384 + i * 64 + row + 8, lanes]
            product = total(at_k(jac_ref, i * NV + j, k) * a[j] for j in range(NV))
            r.append(at_k(source_ref, i, k) - (product - coupled))
        d = [total(at_k(inv_ref, i * NV + j, k) * r[j] for j in range(NV)) for i in range(NV)]
        if k == 0:
            y = d
        else:
            y = [d[i] + total(low_ref[pl.ds((LOW_AT[(i, j)] * KN + k) * 8, 8), :] * y[j] for j in range(i + 1)) for i in range(NV)]
        for i in range(NV):
            drive_ref[pl.ds(i * 128 + k * 8, 8), :] = d[i]
            y_ref[pl.ds(i * 128 + k * 8, 8), :] = y[i]
    u = y
    for k in range(KN - 2, -1, -1):
        u = [
            y_ref[pl.ds(i * 128 + k * 8, 8), :]
            + total(upp_ref[pl.ds((UPP_AT[(i, j)] * KN + k) * 8, 8), :] * u[j] for j in range(i, NV))
            for i in range(NV)
        ]
    for i in range(NV):
        bound_ref[pl.ds(stride - ENDS + i, NQ, stride=stride), :] = y[i]
        bound_ref[pl.ds(stride - ENDS + NV + i, NQ, stride=stride), :] = u[i]


def boundary_kernel(stride, phw_ref, *refs):
    *bounds, out_ref = refs
    bound_ref = bounds[0] if bounds else phw_ref

    def end_at(p, n):
        at = (p + 1) * stride - ENDS + n
        return bound_ref[at : at + 1, :]

    def factor(p, n):
        return phw_ref[p * BOTH + n : p * BOTH + n + 1, :]

    zero = jnp.zeros((1, 128), F32)
    y = [zero] * NV
    entering = []
    for p in range(NQ):
        entering.append(y)
        for i in range(NV):
            out_ref[p * ENDS + i : p * ENDS + i + 1, :] = y[i]
        if p + 1 < NQ:
            y = [
                end_at(p, i)
                + total(factor(p, LOW_AT[(i, j)]) * y[j] for j in range(i + 1))
                for i in range(NV)
            ]
    u = [zero] * NV
    for p in range(NQ - 1, -1, -1):
        for i in range(NV):
            out_ref[p * ENDS + NV + i : p * ENDS + NV + i + 1, :] = u[i]
        if p > 0:
            y = entering[p]
            known = [
                end_at(p, NV + i) + total(factor(p, NP + i * NV + j) * y[j] for j in range(NV))
                for i in range(NV)
            ]
            u = [
                known[i] + total(factor(p, NP + NH + UPP_AT[(i, j)]) * u[j] for j in range(i, NV))
                for i in range(NV)
            ]


def solve_lines(enter_ref, drive_ref, low_ref, upp_ref, cells_ref, y_ref, put):
    y = [enter_ref[pl.ds(i, NQ, stride=ENDS), :] for i in range(NV)]
    u = [enter_ref[pl.ds(NV + i, NQ, stride=ENDS), :] for i in range(NV)]
    for k in range(KN):
        y = [
            drive_ref[pl.ds(i * 128 + k * 8, 8), :]
            + total(low_ref[pl.ds((LOW_AT[(i, j)] * KN + k) * 8, 8), :] * y[j] for j in range(i + 1))
            for i in range(NV)
        ]
        for i in range(NV):
            y_ref[pl.ds(i * 128 + k * 8, 8), :] = y[i]
    for k in range(KN - 1, -1, -1):
        u = [
            y_ref[pl.ds(i * 128 + k * 8, 8), :]
            + total(upp_ref[pl.ds((UPP_AT[(i, j)] * KN + k) * 8, 8), :] * u[j] for j in range(i, NV))
            for i in range(NV)
        ]
        for i in range(NV):
            put(i, k, cells_ref[pl.ds(i * 128 + k * 8, 8), :] + u[i])


def update_kernel(enter_ref, drive_ref, low_ref, upp_ref, cells_ref, send_ref, cycle_ref, out_ref, new_ref, y_ref, x_ref):
    def put(i, k, value):
        new_ref[pl.ds(i * 128 + k * 8, 8), :] = value

    solve_lines(enter_ref, drive_ref, low_ref, upp_ref, cells_ref, y_ref, put)
    gather_all(new_ref, send_ref, cycle_ref, out_ref, x_ref)


def final_kernel(enter_ref, drive_ref, low_ref, upp_ref, cells_ref, new_ref, y_ref):
    def put(i, k, value):
        put_k(new_ref, i, k, value)

    solve_lines(enter_ref, drive_ref, low_ref, upp_ref, cells_ref, y_ref, put)


def f32(*shape):
    return jax.ShapeDtypeStruct(shape, F32)


PARAMS = pltpu.CompilerParams(vmem_limit_bytes=20 * 1024 * 1024)


def body(
    adjoint_start, source, jacobian, inv_diag, lower_prop, upper_prop, send_cells, recv_cells,
    face_weight, cycle_cells, iface_cells, iface_donor, iface_weight,
):
    start = rows_of(adjoint_start)
    src = rows_of(source)
    jac = rows_of(jacobian)
    inv = rows_of(inv_diag)
    low = rows_of(lower_prop)
    upp = rows_of(upper_prop)
    send = send_cells.reshape(NB, 512)
    recv_at = recv_cells.reshape(NB, 512)
    weight = face_weight.reshape(NB, 512)
    cycle = cycle_cells.reshape(1, 512)
    iface_at = iface_cells.reshape(1, 512)
    donor = iface_donor.reshape(2, 512)
    iface_w = iface_weight.reshape(2, 512)

    def call(kernel, name, out, operands, scratch=(), flops=0):
        size = sum(4 * x.size for x in operands)
        return pl.pallas_call(
            kernel,
            out_shape=out,
            in_specs=[VMEM] * len(operands),
            out_specs=jax.tree.map(lambda _: VMEM, out),
            scratch_shapes=list(scratch),
            compiler_params=PARAMS,
            cost_estimate=pl.CostEstimate(flops=flops, bytes_accessed=size, transcendentals=0),
            name=name,
        )(*operands)

    def exchange(x, axis, parts):
        x = x.reshape(parts, x.size // (parts * 128), 128)
        return lax.all_to_all(x, axis, split_axis=0, concat_axis=0, tiled=True)

    field = f32(NV * 128, 128)
    faces = f32(NB, 48, 128)
    table = pltpu.VMEM((768, 256), BF16)
    lines = pltpu.VMEM((NV * 128, 128), F32)
    outgoing, cells = call(first_gather_kernel, "first_gather", (faces, field), (start, send, cycle), [table], PICK)
    for iteration in range(ITERS):
        incoming = exchange(outgoing, "block", NB)
        operands = (recv_at, weight, iface_at, donor, iface_w, cells, src)
        stride = ENDS
        if iteration == 0:
            if ORDER:
                incoming, low, upp = lax.optimization_barrier((incoming, low, upp))
            phw, lowc, uppc = call(
                prepare_kernel,
                "prepare",
                (f32(NQ * ROWS, 128), f32(NP * 128, 128), f32(NP * 128, 128)),
                (low, upp),
                [pltpu.VMEM((KN * NP * 8, 128), F32)],
            )
            stride = BOTH
        operands = (incoming.reshape(NB * 48, 128),) + operands + (lowc, uppc, jac, inv)
        if iteration == 0:
            operands += (phw,)
        bound, drive = call(
            partial(residual_kernel, iteration == 0),
            "residual",
            (f32(NQ * stride, 128), field),
            operands,
            [pltpu.VMEM((768, 256), F32), pltpu.VMEM((768, 128), BF16), lines],
            PICK,
        )
        bound = exchange(bound, "line", NQ).reshape(NQ * stride, 128)
        if iteration == 0:
            products = bound
            operands = (bound,)
        else:
            operands = (products, bound)
        enter = call(partial(boundary_kernel, stride), "boundary", f32(NQ * ENDS, 128), operands)
        enter = exchange(enter, "line", NQ).reshape(NQ * ENDS, 128)
        operands = (enter, drive, lowc, uppc, cells)
        if iteration + 1 < ITERS:
            outgoing, cells = call(update_kernel, "update", (faces, field), operands + (send, cycle), [lines, table], PICK)
        else:
            result = call(final_kernel, "final_update", field, operands, [lines])
    return from_rows(result, NV)[:, None]


def solution(mesh):
    cell = P(None, "block", "line", None)
    matrix = P(None, None, "block", "line", None)
    slots = P("block", "line", None, None)
    flat = P("block", "line", None)
    placed = (cell, cell, matrix, matrix, matrix, matrix, slots, slots, slots, flat, flat, slots, slots)
    return jax.shard_map(body, mesh=mesh, in_specs=placed, out_specs=cell, check_vma=False)
```

time: 140 us -> 98.9 us (0.71)
  blocking collectives: 50.4 us -> 72.4 us
  Pallas kernels: 40.2 us -> 22.5 us
  local copies, waits for them, and re-layouts: 17.3 us -> 3.31 us
  between operations: 13.6 us -> 0.15 us
  waiting for transfers between devices: 9.53 us -> 0 us
  starting transfers between devices: 8.53 us -> 0 us
    all_to_all x3 -> x6, blocking collectives: 50.4 us -> 72.4 us  [exchange(): return lax.all_to_all(x, axis, split_axis=0, concat_axis=0, tiled=True)]
    pallas_call x6 -> x8, Pallas kernels: 40.2 us -> 22.5 us  [call(): pl.pallas_call(kernel, out_shape=out, in_specs=[VMEM] * len(operands), ou...]
    unnamed x54 -> x30, local copies, waits for them, and re-layouts: 17.3 us -> 3.31 us
    all_to_all x1 -> x0, waiting for transfers between devices: 9.52 us -> none  [body(): lax.all_to_all(bound, 'line', split_axis=0, concat_axis=0, tiled=True)]
    all_to_all x1 -> x0, starting transfers between devices: 8.53 us -> none  [body(): lax.all_to_all(bound, 'line', split_axis=0, concat_axis=0, tiled=True)]
  transfers between devices with their start and end apart: 2 -> 0, of which waited for: 1 -> 0; matrix products, arithmetic and copies ran while one was open for 0% -> 0% of each run, Pallas kernels for 13% -> 0%
where the time goes in v1:
time: 98.9 us; the launch traced here: 98.4 us
  blocking collectives  72.4 us (73%)
  Pallas kernels  22.5 us (23%)
  local copies, waits for them, and re-layouts  3.31 us (3%)
    all_to_all x6, blocking collectives, exchange(): return lax.all_to_all(x, axis, split_axis=0, concat_axis=0, tiled=True)  72.4 us
    pallas_call x8, Pallas kernels, call(): pl.pallas_call(kernel, out_shape=out, in_specs=[VMEM] * len(operands), ou...  22.5 us
    unnamed x30, local copies, waits for them, and re-layouts  3.31 us

profile of v1, /device:TPU:0, one launch (start us, length us, event | category | flops | bytes accessed | tf_op | source)
XLA Modules:
  0.0 98.4 jit_solution(4719562907930208208)
XLA Ops:
  0.0 0.0 copy-start.4
  0.0 1.0 %copy-done.4 = f32[6,1,16,1024]{3,2,1,0:T(8,128)S(1)} copy-done((f32[6,1,16,1024]{3,2,1,0:T(8,128)S(1)}, f32[6,1,16,1024]{3,2,1,0:T(8,128)}, u32[]{:S(2)}) %copy-start.4) | copy-done | bytes 393240
  1.0 0.0 copy-start.6
  1.0 0.8 copy-done.6
  1.8 0.0 copy-start.12
  1.8 0.7 copy-done.12
  2.4 0.0 copy-start
  2.4 0.0 copy-start.1
  2.4 4.0 %first_gather.1 = (f32[16,48,128]{2,1,0:T(8,128)S(1)}, f32[768,128]{1,0:T(8,128)S(1)}) custom-call(f32[768,128]{1,0:T(8,128)S(1)} %bitcast.69, s32[16,512]{1,0:T(8,128)S(1)} %bitcast.72, s32[1,512]{1,0:T(1,128)S(1)} %bitcast.82), custom_call_target="tpu_custom_call" | custom-call | flops 3422552064 | bytes 428032 | tf_op jit(solution)/shard_map/first_gather/pallas_call | solution.py:359
  6.4 0.0 copy-start.5
  6.5 0.0 copy-start.8
  6.5 0.0 copy-start.9
  6.5 18.4 %all_to_all.30 = f32[16,48,128]{2,1,0:T(8,128)S(1)} all-to-all(f32[16,48,128]{2,1,0:T(8,128)S(1)} %get-tuple-element.19), channel_id=1, replica_groups=mesh['block'=16,'line'=8] {'block'}, dimensions={0} | all-to-all | bytes 786432 | tf_op jit(solution)/shard_map/all_to_all | solution.py:372
  24.9 0.0 copy-done
  24.9 0.0 copy-done.1
  24.9 0.0 copy-start.2
  24.9 0.0 copy-start.3
  24.9 0.0 copy-start.10
  25.0 0.0 copy-start.11
  25.0 0.0 copy-start.14
  25.0 1.5 %prepare.1 = (f32[640,128]{1,0:T(8,128)S(1)}, f32[2688,128]{1,0:T(8,128)S(1)}, f32[2688,128]{1,0:T(8,128)S(1)}) custom-call(f32[4608,128]{1,0:T(8,128)S(1)} %bitcast.54, f32[4608,128]{1,0:T(8,128)S(1)} %bitcast.55), custom_call_target="tpu_custom_call" | custom-call | bytes 4718592 | tf_op jit(solution)/shard_map/prepare/pallas_call | solution.py:359
  26.5 0.0 copy-done.5
  26.5 0.0 copy-done.8
  26.5 0.0 copy-done.9
  26.5 0.1 copy-done.2
  26.6 0.7 copy-done.3
  27.3 0.0 copy-done.10
  27.3 0.0 copy-done.11
  27.3 0.0 copy-done.14
  27.3 0.0 copy-start.7
  27.3 0.0 copy-start.13
  27.3 5.7 %residual.2 = (f32[768,128]{1,0:T(8,128)S(1)}, f32[768,128]{1,0:T(8,128)S(1)}) custom-call(f32[768,128]{1,0:T(8,128)S(1)} %bitcast.56, s32[16,512]{1,0:T(8,128)S(1)} %bitcast.74, f32[16,512]{1,0:T(8,128)S(1)} %bitcast.76, s32[1,512]{1,0:T(1,128)S(1)} %bitcast.84, s32[2,512]{1,0:T(2,128)S(1)} %bitcast.78, f32[2,512]{1,0:T(2,128)S(1)} %bitcast.80, ...), custom_call_target="tpu_custom_call" | custom-call | flops 3422552064 | bytes 9054208 | tf_op jit(solution)/shard_map/residual/pallas_call | solution.py:359
  33.0 13.0 %all_to_all.31 = f32[8,96,128]{2,1,0:T(8,128)S(1)} all-to-all(f32[8,96,128]{2,1,0:T(8,128)S(1)} %bitcast.57), channel_id=1, replica_groups=mesh['block'=16,'line'=8] {'line'}, dimensions={0} | all-to-all | bytes 786432 | tf_op jit(solution)/shard_map/all_to_all | solution.py:372
  46.1 0.2 boundary.2
  46.2 8.9 %all_to_all.32 = f32[8,16,128]{2,1,0:T(8,128)S(1)} all-to-all(f32[8,16,128]{2,1,0:T(8,128)S(1)} %bitcast.60), channel_id=1, replica_groups=mesh['block'=16,'line'=8] {'line'}, dimensions={0} | all-to-all | bytes 131072 | tf_op jit(solution)/shard_map/all_to_all | solution.py:372
  55.1 0.0 copy-done.7
  55.1 0.0 copy-done.13
  55.1 4.3 %update.1 = (f32[16,48,128]{2,1,0:T(8,128)S(1)}, f32[768,128]{1,0:T(8,128)S(1)}) custom-call(f32[128,128]{1,0:T(8,128)S(1)} %bitcast.63, f32[768,128]{1,0:T(8,128)S(1)} %get-tuple-element.28.drive_ref, f32[2688,128]{1,0:T(8,128)S(1)} %get-tuple-element.24.low_ref, f32[2688,128]{1,0:T(8,128)S(1)} %get-tuple-element.25.upp_ref, ...), custom_call_target="tpu_custom_call" | custom-call | flops 3422552064 | bytes 3639296 | tf_op jit(solution)/shard_map/update/pallas_call | solution.py:359
  59.4 14.6 %all_to_all.33 = f32[16,48,128]{2,1,0:T(8,128)S(1)} all-to-all(f32[16,48,128]{2,1,0:T(8,128)S(1)} %get-tuple-element.29), channel_id=1, replica_groups=mesh['block'=16,'line'=8] {'block'}, dimensions={0} | all-to-all | bytes 786432 | tf_op jit(solution)/shard_map/all_to_all | solution.py:372
  74.0 5.7 %residual.3 = (f32[128,128]{1,0:T(8,128)S(1)}, f32[768,128]{1,0:T(8,128)S(1)}) custom-call(f32[768,128]{1,0:T(8,128)S(1)} %bitcast.58, s32[16,512]{1,0:T(8,128)S(1)} %bitcast.75, f32[16,512]{1,0:T(8,128)S(1)} %bitcast.77, s32[1,512]{1,0:T(1,128)S(1)} %bitcast.85, s32[2,512]{1,0:T(2,128)S(1)} %bitcast.79, f32[2,512]{1,0:T(2,128)S(1)} %bitcast.81, ...), custom_call_target="tpu_custom_call" | custom-call | flops 3422552064 | bytes 8726528 | tf_op jit(solution)/shard_map/residual/pallas_call | solution.py:359
  79.7 8.7 %all_to_all.34 = f32[8,16,128]{2,1,0:T(8,128)S(1)} all-to-all(f32[8,16,128]{2,1,0:T(8,128)S(1)} %bitcast.64), channel_id=1, replica_groups=mesh['block'=16,'line'=8] {'line'}, dimensions={0} | all-to-all | bytes 131072 | tf_op jit(solution)/shard_map/all_to_all | solution.py:372
  88.4 0.2 boundary.3
  88.6 8.8 %all_to_all.35 = f32[8,16,128]{2,1,0:T(8,128)S(1)} all-to-all(f32[8,16,128]{2,1,0:T(8,128)S(1)} %bitcast.62), channel_id=1, replica_groups=mesh['block'=16,'line'=8] {'line'}, dimensions={0} | all-to-all | bytes 131072 | tf_op jit(solution)/shard_map/all_to_all | solution.py:372
  97.3 1.1 %final_update.1 = f32[768,128]{1,0:T(8,128)} custom-call(f32[128,128]{1,0:T(8,128)S(1)} %bitcast.59, f32[768,128]{1,0:T(8,128)S(1)} %get-tuple-element.32.drive_ref, f32[2688,128]{1,0:T(8,128)S(1)} %get-tuple-element.24.low_ref, f32[2688,128]{1,0:T(8,128)S(1)} %get-tuple-element.25.upp_ref, f32[768,128]{1,0:T(8,128)S(1)} %get-tuple-element.30.cells_ref), custom_call_target="tpu_custom_call" | custom-call | bytes 3604480 | tf_op jit(solution)/shard_map/final_update/pallas_call | solution.py:359
Async XLA Ops:
  0.0 1.0 %copy-start.4 = (f32[6,1,16,1024]{3,2,1,0:T(8,128)S(1)}, f32[6,1,16,1024]{3,2,1,0:T(8,128)}, u32[]{:S(2)}) copy-start(f32[6,1,16,1024]{3,2,1,0:T(8,128)} %param.13) | copy-start | bytes 1179652
  1.0 0.8 copy-start.6
  1.8 0.7 copy-start.12
  2.4 22.5 %copy-start = (f32[6,6,1,16,1024]{4,3,2,1,0:T(8,128)S(1)}, f32[6,6,1,16,1024]{4,3,2,1,0:T(8,128)}, u32[]{:S(2)}) copy-start(f32[6,6,1,16,1024]{4,3,2,1,0:T(8,128)} %param.17) | copy-start | bytes 7077892
  2.4 22.5 %copy-start.1 = (f32[6,6,1,16,1024]{4,3,2,1,0:T(8,128)S(1)}, f32[6,6,1,16,1024]{4,3,2,1,0:T(8,128)}, u32[]{:S(2)}) copy-start(f32[6,6,1,16,1024]{4,3,2,1,0:T(8,128)} %param.18) | copy-start | bytes 7077892
  6.4 20.0 %copy-start.5 = (f32[6,1,16,1024]{3,2,1,0:T(8,128)S(1)}, f32[6,1,16,1024]{3,2,1,0:T(8,128)}, u32[]{:S(2)}) copy-start(f32[6,1,16,1024]{3,2,1,0:T(8,128)} %param.14) | copy-start | bytes 1179652
  6.5 20.0 %copy-start.8 = (s32[1,1,16,512]{3,2,1,0:T(8,128)S(1)}, s32[1,1,16,512]{3,2,1,0:T(8,128)}, u32[]{:S(2)}) copy-start(s32[1,1,16,512]{3,2,1,0:T(8,128)} %param.20) | copy-start | bytes 98308
  6.5 20.0 %copy-start.9 = (f32[1,1,16,512]{3,2,1,0:T(8,128)S(1)}, f32[1,1,16,512]{3,2,1,0:T(8,128)}, u32[]{:S(2)}) copy-start(f32[1,1,16,512]{3,2,1,0:T(8,128)} %param.21) | copy-start | bytes 98308
  24.9 1.7 %copy-start.2 = (f32[6,6,1,16,1024]{4,3,2,1,0:T(8,128)S(1)}, f32[6,6,1,16,1024]{4,3,2,1,0:T(8,128)}, u32[]{:S(2)}) copy-start(f32[6,6,1,16,1024]{4,3,2,1,0:T(8,128)} %param.15) | copy-start | bytes 7077892
  24.9 2.4 %copy-start.3 = (f32[6,6,1,16,1024]{4,3,2,1,0:T(8,128)S(1)}, f32[6,6,1,16,1024]{4,3,2,1,0:T(8,128)}, u32[]{:S(2)}) copy-start(f32[6,6,1,16,1024]{4,3,2,1,0:T(8,128)} %param.16) | copy-start | bytes 7077892
  24.9 2.4 %copy-start.10 = (s32[1,1,2,512]{3,2,1,0:T(2,128)S(1)}, s32[1,1,2,512]{3,2,1,0:T(2,128)}, u32[]{:S(2)}) copy-start(s32[1,1,2,512]{3,2,1,0:T(2,128)} %param.24) | copy-start | bytes 12292
  25.0 2.4 %copy-start.11 = (f32[1,1,2,512]{3,2,1,0:T(2,128)S(1)}, f32[1,1,2,512]{3,2,1,0:T(2,128)}, u32[]{:S(2)}) copy-start(f32[1,1,2,512]{3,2,1,0:T(2,128)} %param.25) | copy-start | bytes 12292
  25.0 2.4 %copy-start.14 = (s32[1,1,512]{2,1,0:T(1,128)S(1)}, s32[1,1,512]{2,1,0:T(1,128)}, u32[]{:S(2)}) copy-start(s32[1,1,512]{2,1,0:T(1,128)} %param.23) | copy-start | bytes 6148
  27.3 27.8 %copy-start.7 = (s32[1,1,16,512]{3,2,1,0:T(8,128)S(1)}, s32[1,1,16,512]{3,2,1,0:T(8,128)}, u32[]{:S(2)}) copy-start(s32[1,1,16,512]{3,2,1,0:T(8,128)} %param.19) | copy-start | bytes 98308
  27.3 27.8 %copy-start.13 = (s32[1,1,512]{2,1,0:T(1,128)S(1)}, s32[1,1,512]{2,1,0:T(1,128)}, u32[]{:S(2)}) copy-start(s32[1,1,512]{2,1,0:T(1,128)} %param.22) | copy-start | bytes 6148

commit v2 on v1

--- a/solution.py
+++ b/solution.py
@@ -12,7 +12,7 @@
 NB = 16
 NQ = 8
 ITERS = 2
-ORDER = True
+FIRST_HINT = 6
 PICK = 2 * 768 * 256 * 17 * 512
 F32 = jnp.float32
 BF16 = jnp.bfloat16
@@ -93,15 +93,20 @@
     ]
 
 
-def gather_all(cells_ref, send_ref, cycle_ref, out_ref, x_ref):
+def other_block(me_ref, n):
+    return jnp.bitwise_and(me_ref[0] + 1 + n, NB - 1)
+
+
+def gather_all(me_ref, cells_ref, picks_ref, out_ref, x_ref):
     for v in range(NV):
         stage_table(cells_ref[pl.ds(v * 128, 128), :], x_ref, v, 128)
-    for p in range(NB):
-        got = pick(x_ref, jnp.maximum(send_ref[p : p + 1, :], 0), 128)
+    for n in range(NB - 1):
+        p = other_block(me_ref, n)
+        got = pick(x_ref, jnp.maximum(picks_ref[pl.ds(p, 1), :], 0), 128)
         for v in range(NV):
             for c in range(4):
                 out_ref[p, c * 12 + v : c * 12 + v + 1, :] = got[v][:, c * 128 : (c + 1) * 128]
-    got = pick(x_ref, cycle_ref[...], 128)
+    got = pick(x_ref, picks_ref[NB : NB + 1, :], 128)
     for v in range(NV):
         for c in range(4):
             r = c * 12 + 6 + v
@@ -109,65 +114,57 @@
             out_ref[:, r : r + 1, :] = piece
 
 
-def first_gather_kernel(start_ref, send_ref, cycle_ref, out_ref, cells_ref, x_ref):
+def first_gather_kernel(me_ref, start_ref, picks_ref, out_ref, cells_ref, x_ref):
     for v in range(NV):
         for k in range(KN):
             cells_ref[pl.ds((v * KN + k) * 8, 8), :] = at_k(start_ref, v, k)
-    gather_all(cells_ref, send_ref, cycle_ref, out_ref, x_ref)
-
-
-def prepare_kernel(low_ref, upp_ref, out_ref, lowc_ref, uppc_ref, g_ref):
-    for i, j in LOW:
-        for k in range(KN):
-            lowc_ref[pl.ds((LOW_AT[(i, j)] * KN + k) * 8, 8), :] = at_k(low_ref, i * NV + j, k)
-    for i, j in UPP:
-        for k in range(KN):
-            uppc_ref[pl.ds((UPP_AT[(i, j)] * KN + k) * 8, 8), :] = at_k(upp_ref, i * NV + j, k)
-
-    def low(k, i, j):
-        return lowc_ref[pl.ds((LOW_AT[(i, j)] * KN + k) * 8, 8), :]
-
-    def upp(k, i, j):
-        return uppc_ref[pl.ds((UPP_AT[(i, j)] * KN + k) * 8, 8), :]
-
+    gather_all(me_ref, cells_ref, picks_ref, out_ref, x_ref)
+
+
+def product_steps(low_ref, upp_ref, lowc_ref, uppc_ref, bound_ref, g_ref, h_ref, w_ref):
     def g_at(k, i, j):
         return pl.ds((k * NP + LOW_AT[(i, j)]) * 8, 8)
 
-    def send(n, value):
-        out_ref[pl.ds(n, NQ, stride=ROWS), :] = value
-
-    for j in range(NV):
-        col = {i: low(0, i, j) for i in range(j, NV)}
-        for i in range(j, NV):
-            g_ref[g_at(0, i, j), :] = col[i]
-        for k in range(1, KN):
-            col = {i: total(low(k, i, m) * col[m] for m in range(j, i + 1)) for i in range(j, NV)}
+    def forward_step(k):
+        low = {(i, j): at_k(low_ref, i * NV + j, k) for (i, j) in LOW}
+        for i, j in LOW:
+            lowc_ref[pl.ds((LOW_AT[(i, j)] * KN + k) * 8, 8), :] = low[(i, j)]
+        for j in range(NV):
+            before = {m: g_ref[g_at(k - 1, m, j), :] for m in range(j, NV)} if k else None
             for i in range(j, NV):
-                g_ref[g_at(k, i, j), :] = col[i]
-        for i in range(j, NV):
-            send(LOW_AT[(i, j)], col[i])
-
-    for j in range(NV):
-        hcol = {i: g_ref[g_at(KN - 1, i, j), :] if i >= j else jnp.zeros((8, 128), F32) for i in range(NV)}
-        wcol = {i: upp(KN - 1, i, j) for i in range(j + 1)}
-        for k in range(KN - 2, -1, -1):
-            u = {(i, m): upp(k, i, m) for (i, m) in UPP}
-            wcol = {i: total(u[(i, m)] * wcol[m] for m in range(i, j + 1)) for i in range(j + 1)}
-            new_h = {}
+                g = total(low[(i, m)] * before[m] for m in range(j, i + 1)) if k else low[(i, j)]
+                g_ref[g_at(k, i, j), :] = g
+                if k == KN - 1:
+                    bound_ref[pl.ds(LOW_AT[(i, j)], NQ, stride=BOTH), :] = g
+
+    def backward_step(k):
+        upp = {(i, j): at_k(upp_ref, i * NV + j, k) for (i, j) in UPP}
+        for i, j in UPP:
+            uppc_ref[pl.ds((UPP_AT[(i, j)] * KN + k) * 8, 8), :] = upp[(i, j)]
+        last = k == KN - 1
+        for j in range(NV):
+            old_w = None if last else {m: w_ref[pl.ds(UPP_AT[(m, j)] * 8, 8), :] for m in range(j + 1)}
+            for i in range(j + 1):
+                w = upp[(i, j)] if last else total(upp[(i, m)] * old_w[m] for m in range(i, j + 1))
+                w_ref[pl.ds(UPP_AT[(i, j)] * 8, 8), :] = w
+                if k == 0:
+                    bound_ref[pl.ds(NP + NH + UPP_AT[(i, j)], NQ, stride=BOTH), :] = w
+            old_h = None if last else {m: h_ref[pl.ds((m * NV + j) * 8, 8), :] for m in range(NV)}
             for i in range(NV):
-                terms = [u[(i, m)] * hcol[m] for m in range(i, NV)]
+                terms = [] if last else [upp[(i, m)] * old_h[m] for m in range(i, NV)]
                 if i >= j:
                     terms.append(g_ref[g_at(k, i, j), :])
-                new_h[i] = total(terms)
-            hcol = new_h
-        for i in range(NV):
-            send(NP + i * NV + j, hcol[i])
-        for i in range(j + 1):
-            send(NP + NH + UPP_AT[(i, j)], wcol[i])
+                h = total(terms) if terms else jnp.zeros((8, 128), F32)
+                h_ref[pl.ds((i * NV + j) * 8, 8), :] = h
+                if k == 0:
+                    bound_ref[pl.ds(NP + i * NV + j, NQ, stride=BOTH), :] = h
+
+    return [partial(forward_step, k) for k in range(KN)] + [partial(backward_step, k) for k in range(KN - 1, -1, -1)]
 
 
 def residual_kernel(
     with_products,
+    me_ref,
     recv_ref,
     recv_cells_ref,
     face_weight_ref,
@@ -182,13 +179,14 @@
     inv_ref,
     *refs,
 ):
+    steps = []
     if with_products:
-        products_ref, *refs = refs
-    bound_ref, drive_ref, acc_ref, x_ref, y_ref = refs
+        bound_ref, drive_ref, lowc_ref, uppc_ref, acc_ref, x_ref, y_ref, r_ref, g_ref, h_ref, w_ref = refs
+        steps = product_steps(low_ref, upp_ref, lowc_ref, uppc_ref, bound_ref, g_ref, h_ref, w_ref)
+        low_ref, upp_ref = lowc_ref, uppc_ref
+    else:
+        bound_ref, drive_ref, acc_ref, x_ref, y_ref, r_ref = refs
     stride = BOTH if with_products else ENDS
-    if with_products:
-        for q in range(NQ):
-            bound_ref[q * BOTH : q * BOTH + ROWS, :] = products_ref[q * ROWS : (q + 1) * ROWS, :]
     def add_slots(values, target):
         row = jnp.right_shift(target, 7)
         lane = jnp.bitwise_and(target, 127)
@@ -205,14 +203,26 @@
             left, hot_lane, (((1,), (1,)), ((), ())), preferred_element_type=F32
         )
 
+    def uncoupled(k):
+        a = [cells_ref[pl.ds(v * 128 + k * 8, 8), :] for v in range(NV)]
+        for i in range(NV):
+            product = total(at_k(jac_ref, i * NV + j, k) * a[j] for j in range(NV))
+            r_ref[pl.ds((i * KN + k) * 8, 8), :] = at_k(source_ref, i, k) - product
+
     acc_ref[...] = jnp.zeros_like(acc_ref)
-    for p in range(NB):
-        weight = face_weight_ref[p : p + 1, :]
+    for n in range(NB - 1):
+        p = other_block(me_ref, n)
+        weight = face_weight_ref[pl.ds(p, 1), :]
+        came = recv_ref[pl.ds(pl.multiple_of(p * 48, 8), 48), :]
         values = []
         for v in range(NV):
-            rows = [p * 48 + c * 12 + v for c in range(4)]
-            values.append(jnp.concatenate([recv_ref[r : r + 1, :] for r in rows], axis=1) * weight)
-        add_slots(values, recv_cells_ref[p : p + 1, :])
+            rows = [c * 12 + v for c in range(4)]
+            values.append(jnp.concatenate([came[r : r + 1] for r in rows], axis=1) * weight)
+        add_slots(values, recv_cells_ref[pl.ds(p, 1), :])
+        uncoupled(n)
+        for step in steps[3 * n : 3 * n + 3]:
+            step()
+    uncoupled(KN - 1)
 
     for v in range(NV):
         stage_table(recv_ref[pl.ds(6 + v, 64, stride=12), :], x_ref, v, 64)
@@ -224,15 +234,13 @@
 
     y = None
     for k in range(KN):
-        a = [cells_ref[pl.ds(v * 128 + k * 8, 8), :] for v in range(NV)]
         r = []
         half, row = k // 8, (k % 8) * 8
         lanes = slice(half * 128, half * 128 + 128)
         for i in range(NV):
             coupled = acc_ref[i * 64 + row : i * 64 + row + 8, lanes]
             coupled = coupled + acc_ref[384 + i * 64 + row : 384 + i * 64 + row + 8, lanes]
-            product = total(at_k(jac_ref, i * NV + j, k) * a[j] for j in range(NV))
-            r.append(at_k(source_ref, i, k) - (product - coupled))
+            r.append(r_ref[pl.ds((i * KN + k) * 8, 8), :] + coupled)
         d = [total(at_k(inv_ref, i * NV + j, k) * r[j] for j in range(NV)) for i in range(NV)]
         if k == 0:
             y = d
@@ -314,12 +322,12 @@
             put(i, k, cells_ref[pl.ds(i * 128 + k * 8, 8), :] + u[i])
 
 
-def update_kernel(enter_ref, drive_ref, low_ref, upp_ref, cells_ref, send_ref, cycle_ref, out_ref, new_ref, y_ref, x_ref):
+def update_kernel(me_ref, enter_ref, drive_ref, low_ref, upp_ref, cells_ref, picks_ref, out_ref, new_ref, y_ref, x_ref):
     def put(i, k, value):
         new_ref[pl.ds(i * 128 + k * 8, 8), :] = value
 
     solve_lines(enter_ref, drive_ref, low_ref, upp_ref, cells_ref, y_ref, put)
-    gather_all(new_ref, send_ref, cycle_ref, out_ref, x_ref)
+    gather_all(me_ref, new_ref, picks_ref, out_ref, x_ref)
 
 
 def final_kernel(enter_ref, drive_ref, low_ref, upp_ref, cells_ref, new_ref, y_ref):
@@ -349,17 +357,19 @@
     send = send_cells.reshape(NB, 512)
     recv_at = recv_cells.reshape(NB, 512)
     weight = face_weight.reshape(NB, 512)
-    cycle = cycle_cells.reshape(1, 512)
+    picks = jnp.concatenate([send, cycle_cells.reshape(1, 512)], axis=0)
     iface_at = iface_cells.reshape(1, 512)
     donor = iface_donor.reshape(2, 512)
     iface_w = iface_weight.reshape(2, 512)
+
+    me = lax.axis_index("block").reshape(1).astype(jnp.int32)
 
     def call(kernel, name, out, operands, scratch=(), flops=0):
         size = sum(4 * x.size for x in operands)
         return pl.pallas_call(
             kernel,
             out_shape=out,
-            in_specs=[VMEM] * len(operands),
+            in_specs=[SMEM if x is me else VMEM for x in operands],
             out_specs=jax.tree.map(lambda _: VMEM, out),
             scratch_shapes=list(scratch),
             compiler_params=PARAMS,
@@ -375,33 +385,30 @@
     faces = f32(NB, 48, 128)
     table = pltpu.VMEM((768, 256), BF16)
     lines = pltpu.VMEM((NV * 128, 128), F32)
-    outgoing, cells = call(first_gather_kernel, "first_gather", (faces, field), (start, send, cycle), [table], PICK)
+    outgoing, cells = call(first_gather_kernel, "first_gather", (faces, field), (me, start, picks), [table], FIRST_HINT * PICK)
+    lowc, uppc = low, upp
     for iteration in range(ITERS):
         incoming = exchange(outgoing, "block", NB)
         operands = (recv_at, weight, iface_at, donor, iface_w, cells, src)
         stride = ENDS
+        operands = (me, incoming.reshape(NB * 48, 128)) + operands + (lowc, uppc, jac, inv)
+        scratch = [pltpu.VMEM((768, 256), F32), pltpu.VMEM((768, 128), BF16), lines, lines]
         if iteration == 0:
-            if ORDER:
-                incoming, low, upp = lax.optimization_barrier((incoming, low, upp))
-            phw, lowc, uppc = call(
-                prepare_kernel,
-                "prepare",
-                (f32(NQ * ROWS, 128), f32(NP * 128, 128), f32(NP * 128, 128)),
-                (low, upp),
-                [pltpu.VMEM((KN * NP * 8, 128), F32)],
+            stride = BOTH
+            compact = f32(NP * 128, 128)
+            more = [pltpu.VMEM((KN * NP * 8, 128), F32), pltpu.VMEM((NH * 8, 128), F32), pltpu.VMEM((NP * 8, 128), F32)]
+            bound, drive, lowc, uppc = call(
+                partial(residual_kernel, True),
+                "residual",
+                (f32(NQ * stride, 128), field, compact, compact),
+                operands,
+                scratch + more,
+                PICK,
             )
-            stride = BOTH
-        operands = (incoming.reshape(NB * 48, 128),) + operands + (lowc, uppc, jac, inv)
-        if iteration == 0:
-            operands += (phw,)
-        bound, drive = call(
-            partial(residual_kernel, iteration == 0),
-            "residual",
-            (f32(NQ * stride, 128), field),
-            operands,
-            [pltpu.VMEM((768, 256), F32), pltpu.VMEM((768, 128), BF16), lines],
-            PICK,
-        )
+        else:
+            bound, drive = call(
+                partial(residual_kernel, False), "residual", (f32(NQ * stride, 128), field), operands, scratch, PICK
+            )
         bound = exchange(bound, "line", NQ).reshape(NQ * stride, 128)
         if iteration == 0:
             products = bound
@@ -412,7 +419,7 @@
         enter = exchange(enter, "line", NQ).reshape(NQ * ENDS, 128)
         operands = (enter, drive, lowc, uppc, cells)
         if iteration + 1 < ITERS:
-            outgoing, cells = call(update_kernel, "update", (faces, field), operands + (send, cycle), [lines, table], PICK)
+            outgoing, cells = call(update_kernel, "update", (faces, field), (me,) + operands + (picks,), [lines, table], PICK)
         else:
             result = call(final_kernel, "final_update", field, operands, [lines])
     return from_rows(result, NV)[:, None]

time: 98.9 us -> 96.3 us (0.974)
  local copies, waits for them, and re-layouts: 3.31 us -> 1.05 us
    unnamed x30 -> x22, local copies, waits for them, and re-layouts: 3.31 us -> 1.05 us
    pallas_call x8 -> x7, Pallas kernels: 22.5 us -> 21.6 us  [call(): pl.pallas_call(kernel, out_shape=out, in_specs=[SMEM if x is me else VMEM...]
where the time goes in v2:
time: 96.3 us; the launch traced here: 95.9 us
  blocking collectives  72.3 us (75%)
  Pallas kernels  21.6 us (22%)
  local copies, waits for them, and re-layouts  1.05 us (1%)
    all_to_all x6, blocking collectives, exchange(): return lax.all_to_all(x, axis, split_axis=0, concat_axis=0, tiled=True)  72.3 us
    pallas_call x7, Pallas kernels, call(): pl.pallas_call(kernel, out_shape=out, in_specs=[SMEM if x is me else VMEM...  21.6 us

profile of v2, /device:TPU:0, one launch (start us, length us, event | category | flops | bytes accessed | tf_op | source)
XLA Modules:
  0.0 95.9 jit_solution(5835255054809377139)
XLA Ops:
  0.0 0.8 pad_add_fusion.picks_ref
  0.8 0.0 copy-start.4
  0.8 1.0 %copy-done.4 = f32[6,1,16,1024]{3,2,1,0:T(8,128)S(1)} copy-done((f32[6,1,16,1024]{3,2,1,0:T(8,128)S(1)}, f32[6,1,16,1024]{3,2,1,0:T(8,128)}, u32[]{:S(2)}) %copy-start.4) | copy-done | bytes 393240
  1.8 0.0 copy-start
  1.8 0.0 copy-start.1
  1.8 0.0 copy-start.2
  1.8 0.0 copy-start.3
  1.8 0.0 copy-start.5
  1.8 0.0 copy-start.6
  1.8 0.0 copy-start.7
  1.8 0.0 copy-start.8
  1.8 0.0 copy-start.9
  1.8 0.0 copy-start.10
  1.9 3.8 %first_gather.1 = (f32[16,48,128]{2,1,0:T(8,128)S(1)}, f32[768,128]{1,0:T(8,128)S(1)}) custom-call(s32[1]{0:T(128)} %bitcast.me_ref, f32[768,128]{1,0:T(8,128)S(1)} %bitcast.70, s32[17,512]{1,0:T(8,128)S(1)} %pad_add_fusion.picks_ref), custom_call_target="tpu_custom_call" | custom-call | flops 20535312384 | bytes 428036 | tf_op jit(solution)/shard_map/first_gather/pallas_call | solution.py:369
  5.6 18.3 %all_to_all.30 = f32[16,48,128]{2,1,0:T(8,128)S(1)} all-to-all(f32[16,48,128]{2,1,0:T(8,128)S(1)} %get-tuple-element.15), channel_id=1, replica_groups=mesh['block'=16,'line'=8] {'block'}, dimensions={0} | all-to-all | bytes 786432 | tf_op jit(solution)/shard_map/all_to_all | solution.py:382
  24.0 0.0 copy-done
  24.0 0.0 copy-done.1
  24.0 0.0 copy-done.2
  24.0 0.0 copy-done.3
  24.0 0.0 copy-done.5
  24.0 0.0 copy-done.6
  24.0 0.0 copy-done.7
  24.0 0.0 copy-done.8
  24.0 0.0 copy-done.9
  24.0 0.0 copy-done.10
  24.0 6.9 %residual.2 = (f32[768,128]{1,0:T(8,128)S(1)}, f32[768,128]{1,0:T(8,128)S(1)}, f32[2688,128]{1,0:T(8,128)S(1)}, f32[2688,128]{1,0:T(8,128)S(1)}) custom-call(s32[1]{0:T(128)} %bitcast.me_ref, f32[768,128]{1,0:T(8,128)S(1)} %bitcast.55, s32[16,512]{1,0:T(8,128)S(1)} %bitcast.73, f32[16,512]{1,0:T(8,128)S(1)} %bitcast.75, s32[1,512]{1,0:T(1,128)S(1)} %bitcast.81, ...), custom_call_target="tpu_custom_call" | custom-call | flops 3422552064 | bytes 10692612 | tf_op jit(solution)/shard_map/residual/pallas_call | solution.py:369
  31.0 13.0 %all_to_all.31 = f32[8,96,128]{2,1,0:T(8,128)S(1)} all-to-all(f32[8,96,128]{2,1,0:T(8,128)S(1)} %bitcast.56), channel_id=1, replica_groups=mesh['block'=16,'line'=8] {'line'}, dimensions={0} | all-to-all | bytes 786432 | tf_op jit(solution)/shard_map/all_to_all | solution.py:382
  44.0 0.2 boundary.2
  44.2 8.9 %all_to_all.32 = f32[8,16,128]{2,1,0:T(8,128)S(1)} all-to-all(f32[8,16,128]{2,1,0:T(8,128)S(1)} %bitcast.59), channel_id=1, replica_groups=mesh['block'=16,'line'=8] {'line'}, dimensions={0} | all-to-all | bytes 131072 | tf_op jit(solution)/shard_map/all_to_all | solution.py:382
  53.1 4.1 %update.1 = (f32[16,48,128]{2,1,0:T(8,128)S(1)}, f32[768,128]{1,0:T(8,128)S(1)}) custom-call(s32[1]{0:T(128)} %bitcast.me_ref, f32[128,128]{1,0:T(8,128)S(1)} %bitcast.62, f32[768,128]{1,0:T(8,128)S(1)} %get-tuple-element.18.drive_ref, f32[2688,128]{1,0:T(8,128)S(1)} %get-tuple-element.19.low_ref, f32[2688,128]{1,0:T(8,128)S(1)} %get-tuple-element.20.upp_ref, ...), custom_call_target="tpu_custom_call" | custom-call | flops 3422552064 | bytes 3639300 | tf_op jit(solution)/shard_map/update/pallas_call | solution.py:369
  57.1 14.6 %all_to_all.33 = f32[16,48,128]{2,1,0:T(8,128)S(1)} all-to-all(f32[16,48,128]{2,1,0:T(8,128)S(1)} %get-tuple-element.21), channel_id=1, replica_groups=mesh['block'=16,'line'=8] {'block'}, dimensions={0} | all-to-all | bytes 786432 | tf_op jit(solution)/shard_map/all_to_all | solution.py:382
  71.7 5.4 %residual.3 = (f32[128,128]{1,0:T(8,128)S(1)}, f32[768,128]{1,0:T(8,128)S(1)}) custom-call(s32[1]{0:T(128)} %bitcast.me_ref, f32[768,128]{1,0:T(8,128)S(1)} %bitcast.57, s32[16,512]{1,0:T(8,128)S(1)} %bitcast.74, f32[16,512]{1,0:T(8,128)S(1)} %bitcast.76, s32[1,512]{1,0:T(1,128)S(1)} %bitcast.82, s32[2,512]{1,0:T(2,128)S(1)} %bitcast.78, ...), custom_call_target="tpu_custom_call" | custom-call | flops 3422552064 | bytes 8726532 | tf_op jit(solution)/shard_map/residual/pallas_call | solution.py:369
  77.2 8.7 %all_to_all.34 = f32[8,16,128]{2,1,0:T(8,128)S(1)} all-to-all(f32[8,16,128]{2,1,0:T(8,128)S(1)} %bitcast.63), channel_id=1, replica_groups=mesh['block'=16,'line'=8] {'line'}, dimensions={0} | all-to-all | bytes 131072 | tf_op jit(solution)/shard_map/all_to_all | solution.py:382
  85.9 0.2 boundary.3
  86.0 8.8 %all_to_all.35 = f32[8,16,128]{2,1,0:T(8,128)S(1)} all-to-all(f32[8,16,128]{2,1,0:T(8,128)S(1)} %bitcast.61), channel_id=1, replica_groups=mesh['block'=16,'line'=8] {'line'}, dimensions={0} | all-to-all | bytes 131072 | tf_op jit(solution)/shard_map/all_to_all | solution.py:382
  94.8 1.1 %final_update.1 = f32[768,128]{1,0:T(8,128)} custom-call(f32[128,128]{1,0:T(8,128)S(1)} %bitcast.58, f32[768,128]{1,0:T(8,128)S(1)} %get-tuple-element.24.drive_ref, f32[2688,128]{1,0:T(8,128)S(1)} %get-tuple-element.19.low_ref, f32[2688,128]{1,0:T(8,128)S(1)} %get-tuple-element.20.upp_ref, f32[768,128]{1,0:T(8,128)S(1)} %get-tuple-element.22.cells_ref), custom_call_target="tpu_custom_call" | custom-call | bytes 3604480 | tf_op jit(solution)/shard_map/final_update/pallas_call | solution.py:369
Async XLA Ops:
  0.8 1.0 %copy-start.4 = (f32[6,1,16,1024]{3,2,1,0:T(8,128)S(1)}, f32[6,1,16,1024]{3,2,1,0:T(8,128)}, u32[]{:S(2)}) copy-start(f32[6,1,16,1024]{3,2,1,0:T(8,128)} %param.13) | copy-start | bytes 1179652
  1.8 22.2 %copy-start = (f32[6,6,1,16,1024]{4,3,2,1,0:T(8,128)S(1)}, f32[6,6,1,16,1024]{4,3,2,1,0:T(8,128)}, u32[]{:S(2)}) copy-start(f32[6,6,1,16,1024]{4,3,2,1,0:T(8,128)} %param.17) | copy-start | bytes 7077892
  1.8 22.2 %copy-start.1 = (f32[6,6,1,16,1024]{4,3,2,1,0:T(8,128)S(1)}, f32[6,6,1,16,1024]{4,3,2,1,0:T(8,128)}, u32[]{:S(2)}) copy-start(f32[6,6,1,16,1024]{4,3,2,1,0:T(8,128)} %param.18) | copy-start | bytes 7077892
  1.8 22.2 %copy-start.2 = (f32[6,6,1,16,1024]{4,3,2,1,0:T(8,128)S(1)}, f32[6,6,1,16,1024]{4,3,2,1,0:T(8,128)}, u32[]{:S(2)}) copy-start(f32[6,6,1,16,1024]{4,3,2,1,0:T(8,128)} %param.15) | copy-start | bytes 7077892
  1.8 22.2 %copy-start.3 = (f32[6,6,1,16,1024]{4,3,2,1,0:T(8,128)S(1)}, f32[6,6,1,16,1024]{4,3,2,1,0:T(8,128)}, u32[]{:S(2)}) copy-start(f32[6,6,1,16,1024]{4,3,2,1,0:T(8,128)} %param.16) | copy-start | bytes 7077892
  1.8 22.2 %copy-start.5 = (f32[6,1,16,1024]{3,2,1,0:T(8,128)S(1)}, f32[6,1,16,1024]{3,2,1,0:T(8,128)}, u32[]{:S(2)}) copy-start(f32[6,1,16,1024]{3,2,1,0:T(8,128)} %param.14) | copy-start | bytes 1179652
  1.8 22.2 %copy-start.6 = (s32[1,1,16,512]{3,2,1,0:T(8,128)S(1)}, s32[1,1,16,512]{3,2,1,0:T(8,128)}, u32[]{:S(2)}) copy-start(s32[1,1,16,512]{3,2,1,0:T(8,128)} %param.20) | copy-start | bytes 98308
  1.8 22.2 %copy-start.7 = (f32[1,1,16,512]{3,2,1,0:T(8,128)S(1)}, f32[1,1,16,512]{3,2,1,0:T(8,128)}, u32[]{:S(2)}) copy-start(f32[1,1,16,512]{3,2,1,0:T(8,128)} %param.21) | copy-start | bytes 98308
  1.8 22.2 %copy-start.8 = (s32[1,1,2,512]{3,2,1,0:T(2,128)S(1)}, s32[1,1,2,512]{3,2,1,0:T(2,128)}, u32[]{:S(2)}) copy-start(s32[1,1,2,512]{3,2,1,0:T(2,128)} %param.24) | copy-start | bytes 12292
  1.8 22.2 %copy-start.9 = (f32[1,1,2,512]{3,2,1,0:T(2,128)S(1)}, f32[1,1,2,512]{3,2,1,0:T(2,128)}, u32[]{:S(2)}) copy-start(f32[1,1,2,512]{3,2,1,0:T(2,128)} %param.25) | copy-start | bytes 12292
  1.8 22.2 %copy-start.10 = (s32[1,1,512]{2,1,0:T(1,128)S(1)}, s32[1,1,512]{2,1,0:T(1,128)}, u32[]{:S(2)}) copy-start(s32[1,1,512]{2,1,0:T(1,128)} %param.23) | copy-start | bytes 6148

commit v3 on v2

--- a/solution.py
+++ b/solution.py
@@ -187,7 +187,7 @@
     else:
         bound_ref, drive_ref, acc_ref, x_ref, y_ref, r_ref = refs
     stride = BOTH if with_products else ENDS
-    def add_slots(values, target):
+    def add_slots(values, target, begins=False):
         row = jnp.right_shift(target, 7)
         lane = jnp.bitwise_and(target, 127)
         hot_row = one_hot(jnp.bitwise_and(row, 63), 64)
@@ -199,9 +199,8 @@
         left = jnp.concatenate(
             [hot_row * jnp.concatenate([parts[v][h]] * 4, axis=0) for h in range(2) for v in range(NV)], axis=0
         )
-        acc_ref[...] += lax.dot_general(
-            left, hot_lane, (((1,), (1,)), ((), ())), preferred_element_type=F32
-        )
+        product = lax.dot_general(left, hot_lane, (((1,), (1,)), ((), ())), preferred_element_type=F32)
+        acc_ref[...] = product if begins else acc_ref[...] + product
 
     def uncoupled(k):
         a = [cells_ref[pl.ds(v * 128 + k * 8, 8), :] for v in range(NV)]
@@ -209,7 +208,6 @@
             product = total(at_k(jac_ref, i * NV + j, k) * a[j] for j in range(NV))
             r_ref[pl.ds((i * KN + k) * 8, 8), :] = at_k(source_ref, i, k) - product
 
-    acc_ref[...] = jnp.zeros_like(acc_ref)
     for n in range(NB - 1):
         p = other_block(me_ref, n)
         weight = face_weight_ref[pl.ds(p, 1), :]
@@ -218,9 +216,9 @@
         for v in range(NV):
             rows = [c * 12 + v for c in range(4)]
             values.append(jnp.concatenate([came[r : r + 1] for r in rows], axis=1) * weight)
-        add_slots(values, recv_cells_ref[pl.ds(p, 1), :])
+        add_slots(values, recv_cells_ref[pl.ds(p, 1), :], n == 0)
         uncoupled(n)
-        for step in steps[3 * n : 3 * n + 3]:
+        for step in steps[len(steps) * n // (NB - 1) : len(steps) * (n + 1) // (NB - 1)]:
             step()
     uncoupled(KN - 1)
 

time: 96.3 us -> 96.3 us (level)
  no operation moved by 1% of the time
where the time goes in v3:
time: 96.3 us; the launch traced here: 95.9 us
  blocking collectives  72.3 us (75%)
  Pallas kernels  21.6 us (22%)
  local copies, waits for them, and re-layouts  1.05 us (1%)
    all_to_all x6, blocking collectives, exchange(): return lax.all_to_all(x, axis, split_axis=0, concat_axis=0, tiled=True)  72.3 us
    pallas_call x7, Pallas kernels, call(): pl.pallas_call(kernel, out_shape=out, in_specs=[SMEM if x is me else VMEM...  21.6 us

profile of v3, /device:TPU:0, one launch (start us, length us, event | category | flops | bytes accessed | tf_op | source)
XLA Modules:
  0.0 95.9 jit_solution(6412980346393483564)
XLA Ops:
  0.0 0.8 pad_add_fusion.picks_ref
  0.8 0.0 copy-start.4
  0.8 1.0 %copy-done.4 = f32[6,1,16,1024]{3,2,1,0:T(8,128)S(1)} copy-done((f32[6,1,16,1024]{3,2,1,0:T(8,128)S(1)}, f32[6,1,16,1024]{3,2,1,0:T(8,128)}, u32[]{:S(2)}) %copy-start.4) | copy-done | bytes 393240
  1.8 0.0 copy-start
  1.8 0.0 copy-start.1
  1.8 0.0 copy-start.2
  1.8 0.0 copy-start.3
  1.8 0.0 copy-start.5
  1.8 0.0 copy-start.6
  1.8 0.0 copy-start.7
  1.8 0.0 copy-start.8
  1.8 0.0 copy-start.9
  1.8 0.0 copy-start.10
  1.9 3.8 %first_gather.1 = (f32[16,48,128]{2,1,0:T(8,128)S(1)}, f32[768,128]{1,0:T(8,128)S(1)}) custom-call(s32[1]{0:T(128)} %bitcast.me_ref, f32[768,128]{1,0:T(8,128)S(1)} %bitcast.70, s32[17,512]{1,0:T(8,128)S(1)} %pad_add_fusion.picks_ref), custom_call_target="tpu_custom_call" | custom-call | flops 20535312384 | bytes 428036 | tf_op jit(solution)/shard_map/first_gather/pallas_call | solution.py:367
  5.6 18.3 %all_to_all.30 = f32[16,48,128]{2,1,0:T(8,128)S(1)} all-to-all(f32[16,48,128]{2,1,0:T(8,128)S(1)} %get-tuple-element.15), channel_id=1, replica_groups=mesh['block'=16,'line'=8] {'block'}, dimensions={0} | all-to-all | bytes 786432 | tf_op jit(solution)/shard_map/all_to_all | solution.py:380
  24.0 0.0 copy-done
  24.0 0.0 copy-done.1
  24.0 0.0 copy-done.2
  24.0 0.0 copy-done.3
  24.0 0.0 copy-done.5
  24.0 0.0 copy-done.6
  24.0 0.0 copy-done.7
  24.0 0.0 copy-done.8
  24.0 0.0 copy-done.9
  24.0 0.0 copy-done.10
  24.0 6.9 %residual.2 = (f32[768,128]{1,0:T(8,128)S(1)}, f32[768,128]{1,0:T(8,128)S(1)}, f32[2688,128]{1,0:T(8,128)S(1)}, f32[2688,128]{1,0:T(8,128)S(1)}) custom-call(s32[1]{0:T(128)} %bitcast.me_ref, f32[768,128]{1,0:T(8,128)S(1)} %bitcast.55, s32[16,512]{1,0:T(8,128)S(1)} %bitcast.73, f32[16,512]{1,0:T(8,128)S(1)} %bitcast.75, s32[1,512]{1,0:T(1,128)S(1)} %bitcast.81, ...), custom_call_target="tpu_custom_call" | custom-call | flops 3422552064 | bytes 10692612 | tf_op jit(solution)/shard_map/residual/pallas_call | solution.py:367
  31.0 13.0 %all_to_all.31 = f32[8,96,128]{2,1,0:T(8,128)S(1)} all-to-all(f32[8,96,128]{2,1,0:T(8,128)S(1)} %bitcast.56), channel_id=1, replica_groups=mesh['block'=16,'line'=8] {'line'}, dimensions={0} | all-to-all | bytes 786432 | tf_op jit(solution)/shard_map/all_to_all | solution.py:380
  44.0 0.2 boundary.2
  44.2 8.9 %all_to_all.32 = f32[8,16,128]{2,1,0:T(8,128)S(1)} all-to-all(f32[8,16,128]{2,1,0:T(8,128)S(1)} %bitcast.59), channel_id=1, replica_groups=mesh['block'=16,'line'=8] {'line'}, dimensions={0} | all-to-all | bytes 131072 | tf_op jit(solution)/shard_map/all_to_all | solution.py:380
  53.1 4.1 %update.1 = (f32[16,48,128]{2,1,0:T(8,128)S(1)}, f32[768,128]{1,0:T(8,128)S(1)}) custom-call(s32[1]{0:T(128)} %bitcast.me_ref, f32[128,128]{1,0:T(8,128)S(1)} %bitcast.62, f32[768,128]{1,0:T(8,128)S(1)} %get-tuple-element.18.drive_ref, f32[2688,128]{1,0:T(8,128)S(1)} %get-tuple-element.19.low_ref, f32[2688,128]{1,0:T(8,128)S(1)} %get-tuple-element.20.upp_ref, ...), custom_call_target="tpu_custom_call" | custom-call | flops 3422552064 | bytes 3639300 | tf_op jit(solution)/shard_map/update/pallas_call | solution.py:367
  57.1 14.6 %all_to_all.33 = f32[16,48,128]{2,1,0:T(8,128)S(1)} all-to-all(f32[16,48,128]{2,1,0:T(8,128)S(1)} %get-tuple-element.21), channel_id=1, replica_groups=mesh['block'=16,'line'=8] {'block'}, dimensions={0} | all-to-all | bytes 786432 | tf_op jit(solution)/shard_map/all_to_all | solution.py:380
  71.7 5.4 %residual.3 = (f32[128,128]{1,0:T(8,128)S(1)}, f32[768,128]{1,0:T(8,128)S(1)}) custom-call(s32[1]{0:T(128)} %bitcast.me_ref, f32[768,128]{1,0:T(8,128)S(1)} %bitcast.57, s32[16,512]{1,0:T(8,128)S(1)} %bitcast.74, f32[16,512]{1,0:T(8,128)S(1)} %bitcast.76, s32[1,512]{1,0:T(1,128)S(1)} %bitcast.82, s32[2,512]{1,0:T(2,128)S(1)} %bitcast.78, ...), custom_call_target="tpu_custom_call" | custom-call | flops 3422552064 | bytes 8726532 | tf_op jit(solution)/shard_map/residual/pallas_call | solution.py:367
  77.2 8.7 %all_to_all.34 = f32[8,16,128]{2,1,0:T(8,128)S(1)} all-to-all(f32[8,16,128]{2,1,0:T(8,128)S(1)} %bitcast.63), channel_id=1, replica_groups=mesh['block'=16,'line'=8] {'line'}, dimensions={0} | all-to-all | bytes 131072 | tf_op jit(solution)/shard_map/all_to_all | solution.py:380
  85.9 0.2 boundary.3
  86.0 8.8 %all_to_all.35 = f32[8,16,128]{2,1,0:T(8,128)S(1)} all-to-all(f32[8,16,128]{2,1,0:T(8,128)S(1)} %bitcast.61), channel_id=1, replica_groups=mesh['block'=16,'line'=8] {'line'}, dimensions={0} | all-to-all | bytes 131072 | tf_op jit(solution)/shard_map/all_to_all | solution.py:380
  94.8 1.1 %final_update.1 = f32[768,128]{1,0:T(8,128)} custom-call(f32[128,128]{1,0:T(8,128)S(1)} %bitcast.58, f32[768,128]{1,0:T(8,128)S(1)} %get-tuple-element.24.drive_ref, f32[2688,128]{1,0:T(8,128)S(1)} %get-tuple-element.19.low_ref, f32[2688,128]{1,0:T(8,128)S(1)} %get-tuple-element.20.upp_ref, f32[768,128]{1,0:T(8,128)S(1)} %get-tuple-element.22.cells_ref), custom_call_target="tpu_custom_call" | custom-call | bytes 3604480 | tf_op jit(solution)/shard_map/final_update/pallas_call | solution.py:367
Async XLA Ops:
  0.8 1.0 %copy-start.4 = (f32[6,1,16,1024]{3,2,1,0:T(8,128)S(1)}, f32[6,1,16,1024]{3,2,1,0:T(8,128)}, u32[]{:S(2)}) copy-start(f32[6,1,16,1024]{3,2,1,0:T(8,128)} %param.13) | copy-start | bytes 1179652
  1.8 22.2 %copy-start = (f32[6,6,1,16,1024]{4,3,2,1,0:T(8,128)S(1)}, f32[6,6,1,16,1024]{4,3,2,1,0:T(8,128)}, u32[]{:S(2)}) copy-start(f32[6,6,1,16,1024]{4,3,2,1,0:T(8,128)} %param.17) | copy-start | bytes 7077892
  1.8 22.2 %copy-start.1 = (f32[6,6,1,16,1024]{4,3,2,1,0:T(8,128)S(1)}, f32[6,6,1,16,1024]{4,3,2,1,0:T(8,128)}, u32[]{:S(2)}) copy-start(f32[6,6,1,16,1024]{4,3,2,1,0:T(8,128)} %param.18) | copy-start | bytes 7077892
  1.8 22.2 %copy-start.2 = (f32[6,6,1,16,1024]{4,3,2,1,0:T(8,128)S(1)}, f32[6,6,1,16,1024]{4,3,2,1,0:T(8,128)}, u32[]{:S(2)}) copy-start(f32[6,6,1,16,1024]{4,3,2,1,0:T(8,128)} %param.15) | copy-start | bytes 7077892
  1.8 22.2 %copy-start.3 = (f32[6,6,1,16,1024]{4,3,2,1,0:T(8,128)S(1)}, f32[6,6,1,16,1024]{4,3,2,1,0:T(8,128)}, u32[]{:S(2)}) copy-start(f32[6,6,1,16,1024]{4,3,2,1,0:T(8,128)} %param.16) | copy-start | bytes 7077892
  1.8 22.2 %copy-start.5 = (f32[6,1,16,1024]{3,2,1,0:T(8,128)S(1)}, f32[6,1,16,1024]{3,2,1,0:T(8,128)}, u32[]{:S(2)}) copy-start(f32[6,1,16,1024]{3,2,1,0:T(8,128)} %param.14) | copy-start | bytes 1179652
  1.8 22.2 %copy-start.6 = (s32[1,1,16,512]{3,2,1,0:T(8,128)S(1)}, s32[1,1,16,512]{3,2,1,0:T(8,128)}, u32[]{:S(2)}) copy-start(s32[1,1,16,512]{3,2,1,0:T(8,128)} %param.20) | copy-start | bytes 98308
  1.8 22.2 %copy-start.7 = (f32[1,1,16,512]{3,2,1,0:T(8,128)S(1)}, f32[1,1,16,512]{3,2,1,0:T(8,128)}, u32[]{:S(2)}) copy-start(f32[1,1,16,512]{3,2,1,0:T(8,128)} %param.21) | copy-start | bytes 98308
  1.8 22.2 %copy-start.8 = (s32[1,1,2,512]{3,2,1,0:T(2,128)S(1)}, s32[1,1,2,512]{3,2,1,0:T(2,128)}, u32[]{:S(2)}) copy-start(s32[1,1,2,512]{3,2,1,0:T(2,128)} %param.24) | copy-start | bytes 12292
  1.8 22.2 %copy-start.9 = (f32[1,1,2,512]{3,2,1,0:T(2,128)S(1)}, f32[1,1,2,512]{3,2,1,0:T(2,128)}, u32[]{:S(2)}) copy-start(f32[1,1,2,512]{3,2,1,0:T(2,128)} %param.25) | copy-start | bytes 12292
  1.8 22.2 %copy-start.10 = (s32[1,1,512]{2,1,0:T(1,128)S(1)}, s32[1,1,512]{2,1,0:T(1,128)}, u32[]{:S(2)}) copy-start(s32[1,1,512]{2,1,0:T(1,128)} %param.23) | copy-start | bytes 6148
